TPU v7x, 128 devices: a whole 4x4x4 slice. The times are simulated.
128 devices in a mesh: expert: 16 (over z_hi, y, core), dp: 8 (over x, z_lo).
Axes of the slice: x: 4, y: 4, z: 4 (z_hi: 2, z_lo: 2; z = z_hi * 2 + z_lo), core: 2. Of those that a mesh axis runs over, the one named last changes fastest.
Arguments:
- tokens: bfloat16 [16384, 2048], P(('expert', 'dp')), may hold values from -6 to 6
- cotangent: bfloat16 [16384, 2048], P(('expert', 'dp')), may hold values from -6 to 6
- gate_prob: float32 [16384], P(('expert', 'dp')), may hold values from 0.2 to 1
- expert_of: int32 [16384, 1], P(('expert', 'dp')), may hold values from 0 to 31; in each aligned block of 128 rows (0 to 127, 128 to 255, ...) at most 6 rows name the same one
- w_in: bfloat16 [32, 2048, 5120], P('expert', None, 'dp'), may hold values from -0.125 to 0.125
- w_out: bfloat16 [32, 5120, 2048], P('expert', 'dp'), may hold values from -0.078125 to 0.078125
Outputs:
- layer_out: bfloat16 [16384, 2048], P(('expert', 'dp'))
- grad_in: bfloat16 [32, 2048, 5120], P('expert', None, 'dp')
- grad_out: bfloat16 [32, 5120, 2048], P('expert', 'dp')
Inputs may be any that keep to these rules, and one draw needn't show every extreme that they name: `expert_of`: among one device's 128 tokens no expert is named more than 6 times, and in every draw some device names some expert exactly 6 times.
All inputs are finite; a program needn't handle non-finite values.
Results may differ from a plain program's by a relative error of at most 0.015.
Values may be sent and summed in bfloat16 or wider, within the bound.
A program may use at most 128 MiB of HBM per device.

v0:
```python
import jax
import jax.numpy as jnp
from jax import lax
from jax.sharding import PartitionSpec as P

ROOT = 0.7978845608028654
CUBIC = 0.044715


def gelu_pair(pre_act):
    tanh_arg = ROOT * (pre_act + CUBIC * pre_act * pre_act * pre_act)
    tangent = jnp.tanh(tanh_arg)
    gelu_value = 0.5 * pre_act * (1.0 + tangent)
    gelu_slope = 0.5 * (1.0 + tangent) + 0.5 * pre_act * (1.0 - tangent * tangent) * ROOT * (
        1.0 + 3.0 * CUBIC * pre_act * pre_act
    )
    return (gelu_value, gelu_slope)


def run_expert(rows_x, rows_z, w_first, w_second):
    pre_act = jnp.dot(rows_x, w_first, preferred_element_type=jnp.float32)
    gelu_value, gelu_slope = gelu_pair(pre_act)
    hidden = gelu_value.astype(jnp.bfloat16)
    share_out = jnp.dot(hidden, w_second, preferred_element_type=jnp.float32)
    back_hidden = (
        lax.dot_general(
            rows_z, w_second, (((1,), (1,)), ((), ())), preferred_element_type=jnp.float32
        )
        * gelu_slope
    ).astype(jnp.bfloat16)
    acc_out = lax.dot_general(
        hidden, rows_z, (((0,), (0,)), ((), ())), preferred_element_type=jnp.float32
    )
    acc_in = lax.dot_general(
        rows_x, back_hidden, (((0,), (0,)), ((), ())), preferred_element_type=jnp.float32
    )
    return (share_out, acc_in, acc_out)


def shards(tokens, cotangent, gate_prob, expert_of, w_in, w_out):
    groups = lax.axis_size("expert")
    dp_size = lax.axis_size("dp")
    local_experts = w_in.shape[0]
    model_width = tokens.shape[1]
    tok_dev = tokens.shape[0]
    experts = local_experts * groups
    capacity = max(2, 3 * tok_dev // (2 * experts))
    slot_count = local_experts * capacity
    mine = expert_of[:, 0]
    catalog = jnp.arange(experts, dtype=jnp.int32)
    onehot = (mine[:, None] == catalog[None, :]).astype(jnp.int32)
    rank_in = jnp.sum((jnp.cumsum(onehot, axis=0) - onehot) * onehot, axis=1)
    owner = mine // local_experts
    slot_group = mine % local_experts
    row_of = owner * slot_count + slot_group * capacity + rank_in
    scaled = (gate_prob[:, None] * cotangent.astype(jnp.float32)).astype(jnp.bfloat16)
    send_x = jnp.zeros((groups * slot_count, model_width), jnp.bfloat16).at[row_of].set(tokens)
    send_z = jnp.zeros((groups * slot_count, model_width), jnp.bfloat16).at[row_of].set(scaled)
    wide_x = jnp.broadcast_to(
        send_x.reshape(groups, 1, slot_count, model_width),
        (groups, dp_size, slot_count, model_width),
    ).reshape(-1, model_width)
    wide_z = jnp.broadcast_to(
        send_z.reshape(groups, 1, slot_count, model_width),
        (groups, dp_size, slot_count, model_width),
    ).reshape(-1, model_width)
    got_x, got_z = (
        lax.all_to_all(wide_x, ("expert", "dp"), split_axis=0, concat_axis=0, tiled=True),
        lax.all_to_all(wide_z, ("expert", "dp"), split_axis=0, concat_axis=0, tiled=True),
    )
    senders = got_x.shape[0] // slot_count
    slots_x = got_x.reshape(senders, local_experts, capacity, model_width)
    slots_z = got_z.reshape(senders, local_experts, capacity, model_width)
    outputs = []
    grads_in = []
    grads_out = []
    for slot_index in range(local_experts):
        rows_x = slots_x[:, slot_index].reshape(senders * capacity, model_width)
        rows_z = slots_z[:, slot_index].reshape(senders * capacity, model_width)
        share_out, acc_in, acc_out = run_expert(rows_x, rows_z, w_in[slot_index], w_out[slot_index])
        outputs.append(share_out.reshape(senders, capacity, model_width))
        grads_in.append(acc_in)
        grads_out.append(acc_out)
    partial_value = jnp.stack(outputs, axis=1).reshape(senders * slot_count, model_width)
    total_in = jnp.stack(grads_in)
    total_out = jnp.stack(grads_out)
    returned = lax.all_to_all(
        partial_value.astype(jnp.bfloat16),
        ("expert", "dp"),
        split_axis=0,
        concat_axis=0,
        tiled=True,
    )
    summed = jnp.sum(
        returned.reshape(groups, dp_size, slot_count, model_width).astype(jnp.float32), axis=1
    ).reshape(groups * slot_count, model_width)
    layer_out = (gate_prob[:, None] * summed[row_of]).astype(jnp.bfloat16)
    return (layer_out, total_in.astype(jnp.bfloat16), total_out.astype(jnp.bfloat16))


def solution(mesh):
    return jax.shard_map(
        shards,
        mesh=mesh,
        in_specs=(
            P(("expert", "dp"), None),
            P(("expert", "dp"), None),
            P(("expert", "dp")),
            P(("expert", "dp"), None),
            P("expert", None, "dp"),
            P("expert", "dp", None),
        ),
        out_specs=(P(("expert", "dp"), None), P("expert", None, "dp"), P("expert", "dp", None)),
        check_vma=False,
    )
```

profile of v0, /device:TPU:1, one launch (start us, length us, event | category | flops | bytes accessed | tf_op | source)
XLA Modules:
  0.0 363.4 jit_solution(16439689960888948602)
XLA Ops:
  5.4 4.3 %broadcast_in_dim.9 = bf16[16,8,12,2048]{3,2,1,0:T(8,128)(2,1)} broadcast(bf16[16,12,2048]{2,1,0:T(8,128)(2,1)S(1)} %broadcast_in_dim.8), dimensions={0,2,3} | broadcast | bytes 7077888 | tf_op jit(solution)/shard_map/broadcast_in_dim | solution.py:59
  9.6 12.0 %all-to-all-start = ((bf16[128,12,2048]{2,1,0:T(8,128)(2,1)}), bf16[128,12,2048]{2,1,0:T(8,128)(2,1)}, u32[]{:S(2)}, u32[]{:S(2)}) async-start(bf16[128,12,2048]{2,1,0:T(8,128)(2,1)} %bitcast.90), calls=%async_computation | async-start | bytes 16777216 | tf_op jit(solution)/shard_map/all_to_all | solution.py:68
  23.5 100.1 %all-to-all-done = bf16[128,12,2048]{2,1,0:T(8,128)(2,1)} async-done(((bf16[128,12,2048]{2,1,0:T(8,128)(2,1)}), bf16[128,12,2048]{2,1,0:T(8,128)(2,1)}, u32[]{:S(2)}, u32[]{:S(2)}) %all-to-all-start) | async-done | bytes 6291488 | tf_op jit(solution)/shard_map/all_to_all | solution.py:68
  123.6 4.3 %broadcast_in_dim.11 = bf16[16,8,12,2048]{3,2,1,0:T(8,128)(2,1)} broadcast(bf16[16,12,2048]{2,1,0:T(8,128)(2,1)S(1)} %broadcast_in_dim.10), dimensions={0,2,3} | broadcast | bytes 7077888 | tf_op jit(solution)/shard_map/broadcast_in_dim | solution.py:63
  127.9 9.3 %all-to-all-start.2 = ((bf16[128,12,2048]{2,1,0:T(8,128)(2,1)}), bf16[128,12,2048]{2,1,0:T(8,128)(2,1)}, u32[]{:S(2)}, u32[]{:S(2)}) async-start(bf16[128,12,2048]{2,1,0:T(8,128)(2,1)} %bitcast.89), calls=%async_computation.2 | async-start | bytes 16777216 | tf_op jit(solution)/shard_map/all_to_all | solution.py:69
  137.2 6.8 %copy.19 = bf16[128,12,2048]{2,0,1:T(8,128)(2,1)S(1)} copy(bf16[128,12,2048]{2,1,0:T(8,128)(2,1)} %all-to-all-done) | data formatting | bytes 12582912 | tf_op jit(solution)/shard_map/all_to_all | solution.py:68
  145.2 3.8 %copy.20 = bf16[128,1,6,2048]{3,2,0,1:T(8,128)(2,1)} copy(bf16[128,1,6,2048]{3,0,2,1:T(8,128)(2,1)S(1)} %get-tuple-element.5) | data formatting | bytes 6291456 | tf_op jit(solution)/shard_map/slice | solution.py:78
  148.9 6.3 %reshape_squeeze.12 = bf16[768,2048]{1,0:T(8,128)(2,1)} reshape(bf16[128,1,6,2048]{3,2,0,1:T(8,128)(2,1)} %copy.20) | data formatting | bytes 6291456 | tf_op jit(solution)/shard_map/reshape;squeeze | solution.py:78
  159.0 6.5 %reshape_squeeze.13 = bf16[768,2048]{1,0:T(8,128)(2,1)} reshape(bf16[128,1,6,2048]{3,2,0,1:T(8,128)(2,1)} %copy.22) | data formatting | bytes 6291456 | tf_op jit(solution)/shard_map/reshape;squeeze | solution.py:78
  165.5 6.2 %multiply_convert_fusion.1 = (bf16[768,640]{1,0:T(8,128)(2,1)}, f32[768,640]{1,0:T(8,128)}) fusion(bf16[768,2048]{1,0:T(8,128)(2,1)S(1)} %copy-done, bf16[2,2048,640]{2,1,0:T(8,128)(2,1)} %param.10), kind=kOutput, calls=%fused_computation.54 | convolution fusion | flops 2017689600 | bytes 8716288 | tf_op jit(solution)/shard_map/dot_general | solution.py:21
  173.9 7.0 %multiply_convert_fusion = (bf16[768,640]{1,0:T(8,128)(2,1)}, f32[768,640]{1,0:T(8,128)}) fusion(bf16[768,2048]{1,0:T(8,128)(2,1)} %reshape_squeeze.13, bf16[2,2048,640]{2,1,0:T(8,128)(2,1)} %param.10), kind=kOutput, calls=%fused_computation.53 | convolution fusion | flops 2017689600 | bytes 8716288 | tf_op jit(solution)/shard_map/dot_general | solution.py:21
  183.0 4.6 %fusion = bf16[128,1,6,2048]{3,0,2,1:T(8,128)(2,1)S(1)} fusion(bf16[2,640,2048]{2,1,0:T(8,128)(2,1)} %param.11, bf16[128,6,640]{2,1,0:T(8,128)(2,1)S(1)} %reshape.55), kind=kOutput, calls=%fused_computation.13 | convolution fusion | flops 2014838784 | bytes 6750208 | tf_op jit(solution)/shard_map/dot_general | solution.py:24
  187.6 4.6 %fusion.1 = bf16[128,1,6,2048]{3,0,2,1:T(8,128)(2,1)S(1)} fusion(bf16[2,640,2048]{2,1,0:T(8,128)(2,1)} %param.11, bf16[128,6,640]{2,1,0:T(8,128)(2,1)S(1)} %reshape.56), kind=kOutput, calls=%fused_computation.14 | convolution fusion | flops 2014838784 | bytes 6750208 | tf_op jit(solution)/shard_map/dot_general | solution.py:24
  192.7 6.9 %copy.24 = bf16[128,12,2048]{2,1,0:T(8,128)(2,1)} copy(bf16[128,12,2048]{2,0,1:T(8,128)(2,1)S(1)} %bitcast.93) | data formatting | bytes 12582912 | tf_op jit(solution)/shard_map/convert_element_type | solution.py:88
  199.6 40.1 %all-to-all-done.2 = bf16[128,12,2048]{2,1,0:T(8,128)(2,1)} async-done(((bf16[128,12,2048]{2,1,0:T(8,128)(2,1)}), bf16[128,12,2048]{2,1,0:T(8,128)(2,1)}, u32[]{:S(2)}, u32[]{:S(2)}) %all-to-all-start.2) | async-done | bytes 6291488 | tf_op jit(solution)/shard_map/all_to_all | solution.py:69
  239.7 10.6 %all-to-all-start.1 = ((bf16[128,12,2048]{2,1,0:T(8,128)(2,1)}), bf16[128,12,2048]{2,1,0:T(8,128)(2,1)}, u32[]{:S(2)}, u32[]{:S(2)}) async-start(bf16[128,12,2048]{2,1,0:T(8,128)(2,1)} %copy.24), calls=%async_computation.1 | async-start | bytes 16777216 | tf_op jit(solution)/shard_map/all_to_all | solution.py:87
  250.3 6.8 %copy.27 = bf16[128,12,2048]{2,0,1:T(8,128)(2,1)S(1)} copy(bf16[128,12,2048]{2,1,0:T(8,128)(2,1)} %all-to-all-done.2) | data formatting | bytes 12582912 | tf_op jit(solution)/shard_map/all_to_all | solution.py:69
  262.0 6.3 %reshape_squeeze.14 = bf16[768,2048]{1,0:T(8,128)(2,1)} reshape(bf16[128,1,6,2048]{3,2,0,1:T(8,128)(2,1)} %copy.28) | data formatting | bytes 6291456 | tf_op jit(solution)/shard_map/reshape;squeeze | solution.py:79
  272.1 6.6 %reshape_squeeze.15 = bf16[768,2048]{1,0:T(8,128)(2,1)} reshape(bf16[128,1,6,2048]{3,2,0,1:T(8,128)(2,1)} %copy.29) | data formatting | bytes 6291456 | tf_op jit(solution)/shard_map/reshape;squeeze | solution.py:79
  278.8 11.0 %fusion.2 = bf16[1,2048,640]{2,1,0:T(8,128)(2,1)} fusion(bf16[768,2048]{1,0:T(8,128)(2,1)S(1)} %copy-done.1, f32[768,640]{1,0:T(8,128)} %get-tuple-element.10, bf16[768,2048]{1,0:T(8,128)(2,1)} %reshape_squeeze.14, bf16[2,640,2048]{2,1,0:T(8,128)(2,1)} %param.11), kind=kOutput, calls=%fused_computation.19 | convolution fusion | flops 4037181440 | bytes 13500416 | tf_op jit(solution)/shard_map/dot_general | solution.py:34
  289.8 12.0 %fusion.3 = bf16[1,2048,640]{2,1,0:T(8,128)(2,1)} fusion(bf16[768,2048]{1,0:T(8,128)(2,1)} %reshape_squeeze.13, f32[768,640]{1,0:T(8,128)} %get-tuple-element.8, bf16[768,2048]{1,0:T(8,128)(2,1)} %reshape_squeeze.15, bf16[2,640,2048]{2,1,0:T(8,128)(2,1)} %param.11), kind=kOutput, calls=%fused_computation.20 | convolution fusion | flops 4037181440 | bytes 13500416 | tf_op jit(solution)/shard_map/dot_general | solution.py:34
  301.8 5.0 %pad_maximum_fusion.1 = bf16[2,2048,640]{2,1,0:T(8,128)(2,1)} fusion(bf16[1,2048,640]{2,1,0:T(8,128)(2,1)} %fusion.3, bf16[1,2048,640]{2,1,0:T(8,128)(2,1)S(1)} %copy-done.4), kind=kLoop, calls=%fused_computation.5 | loop fusion | flops 2621440 | bytes 10485760 | tf_op jit(solution)/shard_map/stack | solution.py:85
  314.2 38.6 %all-to-all-done.1 = bf16[128,12,2048]{2,1,0:T(8,128)(2,1)} async-done(((bf16[128,12,2048]{2,1,0:T(8,128)(2,1)}), bf16[128,12,2048]{2,1,0:T(8,128)(2,1)}, u32[]{:S(2)}, u32[]{:S(2)}) %all-to-all-start.1) | async-done | bytes 6291488 | tf_op jit(solution)/shard_map/all_to_all | solution.py:87
  352.9 6.8 %convert_reduce_fusion = f32[16,12,2048]{2,1,0:T(8,128)} fusion(bf16[128,12,2048]{2,1,0:T(8,128)(2,1)} %all-to-all-done.1), kind=kLoop, calls=%fused_computation.3 | loop fusion | flops 5898240 | bytes 7864320 | tf_op jit(solution)/shard_map/reduce_sum | solution.py:94
  (41 shorter events, 35.9 us)
Async XLA Ops:
  9.6 12.0 %copy-start.7 = (bf16[128,2048]{1,0:T(8,128)(2,1)S(1)}, bf16[128,2048]{1,0:T(8,128)(2,1)}, u32[]{:S(2)}) copy-start(bf16[128,2048]{1,0:T(8,128)(2,1)} %param.7) | copy-start | bytes 1572868
  9.6 12.0 %copy-start.8 = (f32[128]{0:T(128)S(1)}, f32[128]{0:T(128)}, u32[]{:S(2)}) copy-start(f32[128]{0:T(128)} %param.8) | copy-start | bytes 1540
  9.6 114.0 %all-to-all-start = ((bf16[128,12,2048]{2,1,0:T(8,128)(2,1)}), bf16[128,12,2048]{2,1,0:T(8,128)(2,1)}, u32[]{:S(2)}, u32[]{:S(2)}) async-start(bf16[128,12,2048]{2,1,0:T(8,128)(2,1)} %bitcast.90), calls=%async_computation | async-start | bytes 16777216 | tf_op jit(solution)/shard_map/all_to_all | solution.py:68
  127.9 111.8 %all-to-all-start.2 = ((bf16[128,12,2048]{2,1,0:T(8,128)(2,1)}), bf16[128,12,2048]{2,1,0:T(8,128)(2,1)}, u32[]{:S(2)}, u32[]{:S(2)}) async-start(bf16[128,12,2048]{2,1,0:T(8,128)(2,1)} %bitcast.89), calls=%async_computation.2 | async-start | bytes 16777216 | tf_op jit(solution)/shard_map/all_to_all | solution.py:69
  159.0 6.5 %copy-start = (bf16[768,2048]{1,0:T(8,128)(2,1)S(1)}, bf16[768,2048]{1,0:T(8,128)(2,1)}, u32[]{:S(2)}) copy-start(bf16[768,2048]{1,0:T(8,128)(2,1)} %reshape_squeeze.12) | copy-start | bytes 9437188
  239.7 113.2 %all-to-all-start.1 = ((bf16[128,12,2048]{2,1,0:T(8,128)(2,1)}), bf16[128,12,2048]{2,1,0:T(8,128)(2,1)}, u32[]{:S(2)}, u32[]{:S(2)}) async-start(bf16[128,12,2048]{2,1,0:T(8,128)(2,1)} %copy.24), calls=%async_computation.1 | async-start | bytes 16777216 | tf_op jit(solution)/shard_map/all_to_all | solution.py:87
  272.1 6.6 %copy-start.1 = (bf16[768,2048]{1,0:T(8,128)(2,1)S(1)}, bf16[768,2048]{1,0:T(8,128)(2,1)}, u32[]{:S(2)}) copy-start(bf16[768,2048]{1,0:T(8,128)(2,1)} %reshape_squeeze.12) | copy-start | bytes 9437188
  289.8 12.0 %copy-start.4 = (bf16[1,2048,640]{2,1,0:T(8,128)(2,1)S(1)}, bf16[1,2048,640]{2,1,0:T(8,128)(2,1)}, u32[]{:S(2)}) copy-start(bf16[1,2048,640]{2,1,0:T(8,128)(2,1)} %fusion.2) | copy-start | bytes 7864324
  301.8 5.0 %copy-start.2 = (bf16[768,2048]{1,0:T(8,128)(2,1)S(1)}, bf16[768,2048]{1,0:T(8,128)(2,1)}, u32[]{:S(2)}) copy-start(bf16[768,2048]{1,0:T(8,128)(2,1)} %reshape_squeeze.14) | copy-start | bytes 9437188
  301.8 5.0 %copy-start.5 = (bf16[768,640]{1,0:T(8,128)(2,1)S(1)}, bf16[768,640]{1,0:T(8,128)(2,1)}, u32[]{:S(2)}) copy-start(bf16[768,640]{1,0:T(8,128)(2,1)} %get-tuple-element.9) | copy-start | bytes 2949124
  306.8 2.3 copy-start.3
  306.8 2.3 copy-start.6
where the time goes:
time: 370 us; the launch traced here: 363 us
  waiting for transfers between devices  179 us (48%)
  local copies, waits for them, and re-layouts  81.5 us (22%)
  matrix products  49.9 us (13%)
  starting transfers between devices  31.8 us (9%)
  other arithmetic  20.2 us (5%)
    all_to_all x1, waiting for transfers between devices, shards(): lax.all_to_all(wide_x, ('expert', 'dp'), split_axis=0, concat_axis=0, til...  100 us
    all_to_all x1, waiting for transfers between devices, shards(): lax.all_to_all(wide_z, ('expert', 'dp'), split_axis=0, concat_axis=0, til...  40.1 us
    all_to_all x1, waiting for transfers between devices, shards(): lax.all_to_all(partial_value.astype(jnp.bfloat16), ('expert', 'dp'), spli...  38.6 us
    dot_general x2, matrix products, run_expert(): lax.dot_general(rows_x, back_hidden, (((0,), (0,)), ((), ())), preferred_...  23 us
    dot_general x2, matrix products, run_expert(): pre_act = jnp.dot(rows_x, w_first, preferred_element_type=jnp.float32)  13.2 us
    another operation x2, local copies, waits for them, and re-layouts, shards(): rows_z = slots_z[:, slot_index].reshape(senders * capacity, model_width)  12.9 us
    another operation x2, local copies, waits for them, and re-layouts, shards(): rows_x = slots_x[:, slot_index].reshape(senders * capacity, model_width)  12.8 us
    all_to_all x1, starting transfers between devices, shards(): lax.all_to_all(wide_x, ('expert', 'dp'), split_axis=0, concat_axis=0, til...  12 us
  transfers between devices with their start and end apart: 3, of which 3 were waited for; matrix products, arithmetic and copies ran while one was open for 35% of the time, Pallas kernels for 0%

commit v1 on v0

v1 whole, which is shorter than its diff:
```python
import functools

import jax
import jax.numpy as jnp
import numpy as np
from jax import lax
from jax.experimental import pallas as pl
from jax.experimental.pallas import tpu as pltpu
from jax.sharding import PartitionSpec as P

ROOT = 0.7978845608028654
CUBIC = 0.044715
BF = jnp.bfloat16
F32 = jnp.float32
MESH = pl.DeviceIdType.MESH
CAP = 6
LOCAL = 2
SLOT = 16
NG = 16
NX = 4
ND = 8
HALF = NG * CAP
ROWS = LOCAL * HALF

AG = ("z1", "z20", "z2m", "z2p", "z22", "xp1", "xm1", "xp2", "xm2", "xp1z", "xm1z",
      "fp1", "fm1", "fp2", "fm2", "fp1z", "fm1z")
RS = ("a0", "a1", "b0", "b1", "c0", "c1", "d0", "d1", "z", "q0", "q1", "q2", "q3",
      "s0", "s1", "t0", "t1")


def gelu_pair(p):
    s = jnp.tanh(ROOT * (p + CUBIC * p * p * p))
    value = 0.5 * p * (1.0 + s)
    slope = 0.5 * (1.0 + s) + 0.5 * p * (1.0 - s * s) * ROOT * (1.0 + 3.0 * CUBIC * p * p)
    return value, slope


def dot(a, b):
    return jnp.dot(a, b, preferred_element_type=F32)


def dot_nt(a, b):
    return lax.dot_general(a, b, (((1,), (1,)), ((), ())), preferred_element_type=F32)


def dot_tn(a, b):
    return lax.dot_general(a, b, (((0,), (0,)), ((), ())), preferred_element_type=F32)


def kernel(
    c1, c2,
    tok_ref, cot_ref, gate_ref, ecol_ref, erow_ref, pack_ref, spread_ref, win_hbm, wout_hbm,
    out_ref, gin_hbm, gout_hbm,
    sx1, sx2, sc1, sc2, ax1, ax2, ac1, ac2,
    gx1, gx2, gc1, gc2,
    win, wout, hid, slp, bh, p1, p2,
    ra, rb, rc, rd, rz, q1, qs0, qs1, qt0, qt1, zout,
    ret1, ret2, back1, back2,
    wsem, a_send, a_recv, g_send, g_recv, r_send, r_recv,
):
    e = lax.axis_index("expert")
    d = lax.axis_index("dp")
    zhi = e // 8
    x = d // 2
    zlo = d % 2
    zot = 1 - zlo
    xr = (x + 1) % NX
    xl = (x + 3) % NX
    xf = (x + 2) % NX
    zp = x * 2 + zot
    dxr = xr * 2 + zlo
    dxl = xl * 2 + zlo
    right, left, pair = (e, dxr), (e, dxl), (e, zp)

    def group_dev(g):
        cross = (zhi + g // 8) % 2
        return (g, x * 2 + (zlo + cross) % 2)

    load_in = pltpu.make_async_copy(win_hbm, win, wsem.at[0])
    load_out = pltpu.make_async_copy(wout_hbm, wout, wsem.at[1])
    load_in.start()
    load_out.start()

    bar = pltpu.get_barrier_semaphore()

    def greet(k, carry):
        pl.semaphore_signal(bar, inc=1, device_id=group_dev((e + k) % NG), device_id_type=MESH)
        return carry

    lax.fori_loop(1, NG, greet, 0)
    for dev in (right, left, pair):
        pl.semaphore_signal(bar, inc=1, device_id=dev, device_id_type=MESH)

    n_tok = tok_ref.shape[0]
    n_exp = NG * LOCAL
    erow = erow_ref[...]
    one_row = (lax.broadcasted_iota(jnp.int32, (n_exp, n_tok), 0) == erow).astype(F32)
    before_row = (
        lax.broadcasted_iota(jnp.int32, (n_tok, n_tok), 0)
        < lax.broadcasted_iota(jnp.int32, (n_tok, n_tok), 1)
    ).astype(F32)
    rank_row = jnp.sum(dot(one_row.astype(BF), before_row.astype(BF)) * one_row, axis=0, keepdims=True)
    slot_row = (erow >> 1) * SLOT + (erow & 1) * CAP + rank_row.astype(jnp.int32)
    ecol = ecol_ref[...]
    one_col = (lax.broadcasted_iota(jnp.int32, (n_tok, n_exp), 1) == ecol).astype(F32)
    before_col = (
        lax.broadcasted_iota(jnp.int32, (n_tok, n_tok), 1)
        < lax.broadcasted_iota(jnp.int32, (n_tok, n_tok), 0)
    ).astype(F32)
    rank_col = jnp.sum(dot(before_col.astype(BF), one_col.astype(BF)) * one_col, axis=1, keepdims=True)
    slot_col = (ecol >> 1) * SLOT + (ecol & 1) * CAP + rank_col.astype(jnp.int32)
    n_slot = NG * SLOT
    put = (lax.broadcasted_iota(jnp.int32, (n_slot, n_tok), 0) == slot_row).astype(F32).astype(BF)

    def fill(dst, acc_dst, value):
        dst[...] = value.astype(BF).reshape(dst.shape)
        acc_dst[pl.ds(e, 1)] = dst[pl.ds(e, 1)]

    def scatter_out(j, src, dst):
        def go(k, carry):
            g = (e + k) % NG
            pltpu.make_async_remote_copy(
                src_ref=src.at[g], dst_ref=dst.at[e], send_sem=a_send.at[j, k], recv_sem=a_recv.at[j, k],
                device_id=group_dev(g), device_id_type=MESH,
            ).start()
            return carry

        lax.fori_loop(1, NG, go, 0)

    def scatter_in(j, src, dst):
        def go(k, carry):
            g = (e + NG - k) % NG
            pltpu.make_async_remote_copy(
                src_ref=src.at[g], dst_ref=dst.at[g], send_sem=a_send.at[j, k], recv_sem=a_recv.at[j, k],
                device_id=group_dev(g), device_id_type=MESH,
            ).wait_recv()
            return carry

        lax.fori_loop(1, NG, go, 0)

    def scatter_sent(j, src, dst):
        def go(k, carry):
            g = (e + k) % NG
            pltpu.make_async_remote_copy(
                src_ref=src.at[g], dst_ref=dst.at[e], send_sem=a_send.at[j, k], recv_sem=a_recv.at[j, k],
                device_id=group_dev(g), device_id_type=MESH,
            ).wait_send()
            return carry

        lax.fori_loop(1, NG, go, 0)

    fill(sx1, ax1, dot(put, tok_ref[:, :c1]))
    pl.semaphore_wait(bar, NG - 1 + 3)
    scatter_out(0, sx1, ax1)
    fill(sx2, ax2, dot(put, tok_ref[:, c1:]))
    scatter_out(1, sx2, ax2)
    gate = gate_ref[...]
    fill(sc1, ac1, dot(put, (gate * cot_ref[:, :c1].astype(F32)).astype(BF)))
    scatter_out(2, sc1, ac1)
    fill(sc2, ac2, dot(put, (gate * cot_ref[:, c1:].astype(F32)).astype(BF)))
    scatter_out(3, sc2, ac2)

    pack = pack_ref[...]

    def compact(j, src, arrived, g):
        scatter_in(j, src, arrived)
        rows = arrived[...].reshape(n_slot, arrived.shape[-1])
        g[pl.ds(d, 1)] = dot(pack, rows).astype(BF).reshape(1, ROWS, arrived.shape[-1])

    sent = []

    def go(sems, names, name, src, dst, dev):
        i = names.index(name)
        cp = pltpu.make_async_remote_copy(
            src_ref=src, dst_ref=dst, send_sem=sems[0].at[i], recv_sem=sems[1].at[i], device_id=dev, device_id_type=MESH
        )
        cp.start()
        sent.append(cp)

    def got(sems, names, name, dst):
        i = names.index(name)
        pltpu.make_async_remote_copy(
            src_ref=dst, dst_ref=dst, send_sem=sems[0].at[i], recv_sem=sems[1].at[i], device_id=pair, device_id_type=MESH
        ).wait_recv()

    lo, hi = pl.ds(0, HALF), pl.ds(HALF, HALF)

    class Gather:
        def __init__(self, i, g1, g2):
            self.sems = (g_send.at[i], g_recv.at[i])
            self.g1, self.g2 = g1, g2

        def go(self, name, ref, dev):
            go(self.sems, AG, name, ref, ref, dev)

        def got(self, name, ref):
            got(self.sems, AG, name, ref)

        def own1(self):
            g1 = self.g1
            self.go("z1", g1.at[d], pair)
            self.go("xp1", g1.at[d], right)
            self.go("xm1", g1.at[d], left)

        def own2(self):
            g2 = self.g2
            self.go("xp2", g2.at[d], right)
            self.go("xm2", g2.at[d], left)
            self.go("z20", g2.at[d], pair)

        def first(self):
            g1 = self.g1
            self.got("z1", g1.at[zp])
            self.go("xp1z", g1.at[zp], right)
            self.go("xm1z", g1.at[zp], left)
            self.got("xp1", g1.at[dxl])
            self.go("fp1", g1.at[dxl, lo], right)
            self.got("xm1", g1.at[dxr])
            self.go("fm1", g1.at[dxr, hi], left)

        def second(self):
            g2 = self.g2
            self.got("xp2", g2.at[dxl])
            self.go("fp2", g2.at[dxl, lo], right)
            self.go("z2m", g2.at[dxl], pair)
            self.got("xm2", g2.at[dxr])
            self.go("fm2", g2.at[dxr, hi], left)
            self.go("z2p", g2.at[dxr], pair)

        def near(self):
            self.got("z20", self.g2.at[zp])

        def third(self):
            g1 = self.g1
            self.got("xp1z", g1.at[xl * 2 + zot])
            self.go("fp1z", g1.at[xl * 2 + zot, lo], right)
            self.got("xm1z", g1.at[xr * 2 + zot])
            self.go("fm1z", g1.at[xr * 2 + zot, hi], left)

        def fourth(self):
            g2 = self.g2
            self.got("fp2", g2.at[xf * 2 + zlo, lo])
            self.got("fm2", g2.at[xf * 2 + zlo, hi])
            self.go("z22", g2.at[xf * 2 + zlo], pair)

        def left_done(self):
            self.got("z2m", self.g2.at[xl * 2 + zot])

        def right_done(self):
            self.got("z2p", self.g2.at[xr * 2 + zot])

        def far_done(self):
            g1 = self.g1
            self.got("fp1", g1.at[xf * 2 + zlo, lo])
            self.got("fm1", g1.at[xf * 2 + zlo, hi])
            self.got("fp1z", g1.at[xf * 2 + zot, lo])
            self.got("fm1z", g1.at[xf * 2 + zot, hi])
            self.got("z22", self.g2.at[xf * 2 + zot])

    def block(ref, xi, le):
        return ref[pl.ds(2 * xi, 2), pl.ds(pl.multiple_of(le * HALF, 32), HALF), :].reshape(2 * HALF, ref.shape[-1])

    def keep(ref, xi, le, value):
        ref[pl.ds(2 * xi, 2), pl.ds(pl.multiple_of(le * HALF, 32), HALF), :] = value.reshape(2, HALF, ref.shape[-1])

    def forward(xi):
        def one(le, carry):
            pre = dot(block(gx1, xi, le), win[le, :c1, :]) + dot(block(gx2, xi, le), win[le, c1:, :])
            value, slope = gelu_pair(pre)
            h = value.astype(BF)
            keep(hid, xi, le, h)
            keep(slp, xi, le, slope)
            keep(p1, xi, le, dot(h, wout[le, :, :c1]).astype(BF))
            keep(p2, xi, le, dot(h, wout[le, :, c1:]).astype(BF))
            return carry

        lax.fori_loop(0, LOCAL, one, 0)

    def backward(xi):
        def one(le, carry):
            b = dot_nt(block(gc1, xi, le), wout[le, :, :c1]) + dot_nt(block(gc2, xi, le), wout[le, :, c1:])
            keep(bh, xi, le, (b * block(slp, xi, le)).astype(BF))
            return carry

        lax.fori_loop(0, LOCAL, one, 0)

    def rows_of(ref, le, start, size):
        return ref[:, pl.ds(pl.multiple_of(le * HALF, 32), HALF), pl.ds(start, size)].reshape(ND * HALF, size)

    TILE = 128

    def grads_in(le):
        bhe = rows_of(bh, le, 0, bh.shape[-1])

        def first(i, carry):
            s = pl.multiple_of(i * TILE, TILE)
            win[le, pl.ds(s, TILE), :] = dot_tn(rows_of(gx1, le, s, TILE), bhe).astype(BF)
            return carry

        def second(i, carry):
            s = pl.multiple_of(i * TILE, TILE)
            win[le, pl.ds(c1 + s, TILE), :] = dot_tn(rows_of(gx2, le, s, TILE), bhe).astype(BF)
            return carry

        lax.fori_loop(0, c1 // TILE, first, 0)
        lax.fori_loop(0, c2 // TILE, second, 0)

    def grads_out(le):
        def one(i, carry):
            s = pl.multiple_of(i * TILE, TILE)
            h = rows_of(hid, le, s, TILE)
            wout[le, pl.ds(s, TILE), :c1] = dot_tn(h, rows_of(gc1, le, 0, c1)).astype(BF)
            wout[le, pl.ds(s, TILE), c1:] = dot_tn(h, rows_of(gc2, le, 0, c2)).astype(BF)
            return carry

        lax.fori_loop(0, hid.shape[-1] // TILE, one, 0)

    rsems = (r_send, r_recv)

    def rgo(name, src, dst, dev):
        go(rsems, RS, name, src, dst, dev)

    def rgot(name, dst):
        got(rsems, RS, name, dst)

    def add(dst, src):
        dst[...] = (dst[...].astype(F32) + src[...].astype(F32)).astype(BF)

    zs = ((0, zlo), (1, zot))

    X, C = Gather(0, gx1, gx2), Gather(1, gc1, gc2)
    compact(0, sx1, ax1, gx1)
    X.own1()
    compact(1, sx2, ax2, gx2)
    X.own2()
    compact(2, sc1, ac1, gc1)
    compact(3, sc2, ac2, gc2)
    X.first()
    X.second()
    X.near()
    load_in.wait()
    load_out.wait()
    forward(x)
    C.own1()
    C.own2()
    X.third()
    X.fourth()
    X.left_done()
    forward(xl)
    X.right_done()
    forward(xr)
    C.first()
    C.second()
    X.far_done()
    forward(xf)
    for j, z in zs:
        rgo(f"a{j}", p1.at[xf * 2 + z, lo], ra.at[j], right)
        rgo(f"b{j}", p1.at[xf * 2 + z, hi], rb.at[j], left)
    for j, xi in enumerate((xf, xl, xr, x)):
        rgo(f"q{j}", p2.at[xi * 2 + zot], q1.at[j], pair)
    C.near()
    backward(x)
    C.third()
    C.fourth()
    C.left_done()
    backward(xl)
    C.right_done()
    backward(xr)
    for j, z in zs:
        rgot(f"a{j}", ra.at[j])
        add(p1.at[xr * 2 + z, lo], ra.at[j])
        rgo(f"c{j}", p1.at[xr * 2 + z], rc.at[j], right)
        rgot(f"b{j}", rb.at[j])
        add(p1.at[xl * 2 + z, hi], rb.at[j])
        rgo(f"d{j}", p1.at[xl * 2 + z], rd.at[j], left)
    for j, xi in enumerate((xf, xl, xr, x)):
        rgot(f"q{j}", q1.at[j])
        add(p2.at[xi * 2 + zlo], q1.at[j])
        if j == 0:
            rgo("s0", p2.at[xf * 2 + zlo, lo], qs0, right)
            rgo("s1", p2.at[xf * 2 + zlo, hi], qs1, left)
    C.far_done()
    backward(xf)
    grads_in(0)
    rgot("s0", qs0)
    add(p2.at[xr * 2 + zlo, lo], qs0)
    rgo("t0", p2.at[xr * 2 + zlo], qt0, right)
    rgot("s1", qs1)
    add(p2.at[xl * 2 + zlo, hi], qs1)
    rgo("t1", p2.at[xl * 2 + zlo], qt1, left)
    rgot("c1", rc.at[1])
    rgot("d1", rd.at[1])
    zout[...] = (p1[zp].astype(F32) + rc[1].astype(F32) + rd[1].astype(F32)).astype(BF)
    rgo("z", zout, rz, pair)
    grads_in(1)
    save_in = pltpu.make_async_copy(win, gin_hbm, wsem.at[0])
    save_in.start()
    grads_out(0)
    grads_out(1)
    save_out = pltpu.make_async_copy(wout, gout_hbm, wsem.at[1])
    save_out.start()
    spread = spread_ref[...]
    rgot("t0", qt0)
    rgot("t1", qt1)
    total = p2[d].astype(F32) + qt0[...].astype(F32) + qt1[...].astype(F32)
    fill(ret2, back2, dot(spread, total.astype(BF)))
    scatter_out(4, ret2, back2)
    rgot("c0", rc.at[0])
    rgot("d0", rd.at[0])
    rgot("z", rz)
    total = p1[d].astype(F32) + rc[0].astype(F32) + rd[0].astype(F32) + rz[...].astype(F32)
    fill(ret1, back1, dot(spread, total.astype(BF)))
    scatter_out(5, ret1, back1)
    take = (lax.broadcasted_iota(jnp.int32, (n_tok, n_slot), 1) == slot_col).astype(F32).astype(BF)
    scatter_in(4, ret2, back2)
    out_ref[:, c1:] = (gate * dot(take, back2[...].reshape(n_slot, c2))).astype(BF)
    scatter_in(5, ret1, back1)
    out_ref[:, :c1] = (gate * dot(take, back1[...].reshape(n_slot, c1))).astype(BF)

    for j, (src, dst) in enumerate(((sx1, ax1), (sx2, ax2), (sc1, ac1), (sc2, ac2), (ret2, back2), (ret1, back1))):
        scatter_sent(j, src, dst)
    for cp in sent:
        cp.wait_send()
    save_in.wait()
    save_out.wait()


def shards(tokens, cotangent, gate_prob, expert_of, w_in, w_out):
    n_tok, width = tokens.shape
    ff = w_in.shape[-1]
    c1 = width * 9 // 16
    c2 = width - c1
    o = np.arange(ROWS)
    source = (o % HALF) // CAP * SLOT + o // HALF * CAP + o % CAP
    pack = (np.arange(NG * SLOT)[None, :] == source[:, None]).astype(np.float32)
    vm = pl.BlockSpec(memory_space=pltpu.VMEM)
    hbm = pl.BlockSpec(memory_space=pl.ANY)

    def buf(*shape):
        return pltpu.VMEM(shape, BF)

    slots = [buf(NG, SLOT, c1), buf(NG, SLOT, c2)]
    gathered = [buf(ND, ROWS, c1), buf(ND, ROWS, c2)]
    return pl.pallas_call(
        functools.partial(kernel, c1, c2),
        out_shape=(
            jax.ShapeDtypeStruct(tokens.shape, BF),
            jax.ShapeDtypeStruct(w_in.shape, BF),
            jax.ShapeDtypeStruct(w_out.shape, BF),
        ),
        in_specs=[vm] * 7 + [hbm] * 2,
        out_specs=(vm, hbm, hbm),
        scratch_shapes=[
            *slots, *slots, *slots, *slots,
            *gathered, *gathered,
            buf(*w_in.shape), buf(*w_out.shape),
            buf(ND, ROWS, ff), pltpu.VMEM((ND, ROWS, ff), F32), buf(ND, ROWS, ff),
            *gathered,
            buf(2, HALF, c1), buf(2, HALF, c1), buf(2, ROWS, c1), buf(2, ROWS, c1), buf(ROWS, c1),
            buf(NX, ROWS, c2), buf(HALF, c2), buf(HALF, c2), buf(ROWS, c2), buf(ROWS, c2), buf(ROWS, c1),
            *slots, *slots,
            pltpu.SemaphoreType.DMA((2,)),
            pltpu.SemaphoreType.DMA((6, NG)), pltpu.SemaphoreType.DMA((6, NG)),
            pltpu.SemaphoreType.DMA((2, len(AG))), pltpu.SemaphoreType.DMA((2, len(AG))),
            pltpu.SemaphoreType.DMA((len(RS),)), pltpu.SemaphoreType.DMA((len(RS),)),
        ],
        compiler_params=pltpu.CompilerParams(collective_id=0, has_side_effects=True, vmem_limit_bytes=62 << 20),
        cost_estimate=pl.CostEstimate(
            flops=10 * ND * ROWS * width * ff, bytes_accessed=8 * w_in.size, transcendentals=ND * ROWS * ff
        ),
    )(
        tokens, cotangent, gate_prob[:, None], expert_of, expert_of.reshape(1, n_tok),
        jnp.asarray(pack, BF), jnp.asarray(pack.T, BF), w_in, w_out,
    )


def solution(mesh):
    return jax.shard_map(
        shards,
        mesh=mesh,
        in_specs=(
            P(("expert", "dp"), None),
            P(("expert", "dp"), None),
            P(("expert", "dp")),
            P(("expert", "dp"), None),
            P("expert", None, "dp"),
            P("expert", "dp", None),
        ),
        out_specs=(P(("expert", "dp"), None), P("expert", None, "dp"), P("expert", "dp", None)),
        check_vma=False,
    )
```

time: 370 us -> 183 us (0.49); the launches traced: 363 us -> 183 us
  waiting for transfers between devices: 179 us -> 0 us
  Pallas kernels: 0 us -> 170 us
  local copies, waits for them, and re-layouts: 81.5 us -> 12.6 us
  matrix products: 49.9 us -> 0 us
  starting transfers between devices: 31.8 us -> 0 us
  other arithmetic: 20.2 us -> 0.01 us
    all_to_all x3 -> x0, waiting for transfers between devices: 179 us -> none  [the longest x1 100 us: shards(): lax.all_to_all(wide_x, ('expert', 'dp'), split_axis=0, concat_axis=0, til...]
    pallas_call x0 -> x1, Pallas kernels: none -> 170 us  [shards(): pl.pallas_call(functools.partial(kernel, c1, c2), out_shape=(jax.ShapeDty...]
    dot_general x8 -> x0, matrix products: 49.9 us -> none  [the longest x2 23 us: run_expert(): lax.dot_general(rows_x, back_hidden, (((0,), (0,)), ((), ())), preferred_...]
    all_to_all x3 -> x0, starting transfers between devices: 31.8 us -> none  [the longest x1 12 us: shards(): lax.all_to_all(wide_x, ('expert', 'dp'), split_axis=0, concat_axis=0, til...]
    another operation x6 -> x0, local copies, waits for them, and re-layouts: 30.1 us -> none  [the longest x2 12.9 us: shards(): rows_z = slots_z[:, slot_index].reshape(senders * capacity, model_width)]
    slice x6 -> x0, local copies, waits for them, and re-layouts: 17.3 us -> none  [the longest x3 8.66 us: shards(): rows_x = slots_x[:, slot_index].reshape(senders * capacity, model_width)]
    all_to_all x2 -> x0, local copies, waits for them, and re-layouts: 13.7 us -> none  [the longest x1 6.83 us: shards(): lax.all_to_all(wide_x, ('expert', 'dp'), split_axis=0, concat_axis=0, til...]
    unnamed x18 -> x8, local copies, waits for them, and re-layouts: 0.03 us -> 11.2 us
  transfers between devices with their start and end apart: 3 -> 0, of which waited for: 3 -> 0; matrix products, arithmetic and copies ran while one was open for 35% -> 0% of each run, Pallas kernels for 0% -> 0%
where the time goes in v1:
time: 183 us
  Pallas kernels  170 us (93%)
  local copies, waits for them, and re-layouts  12.6 us (7%)
    pallas_call x1, Pallas kernels, shards(): pl.pallas_call(functools.partial(kernel, c1, c2), out_shape=(jax.ShapeDty...  170 us
    unnamed x8, local copies, waits for them, and re-layouts  11.2 us

profile of v1, /device:TPU:1, one launch (start us, length us, event | category | flops | bytes accessed | tf_op | source)
XLA Modules:
  0.0 183.1 jit_solution(17004426876808541748)
XLA Ops:
  0.6 1.4 copy.11.gate_ref
  2.0 1.4 copy.12.ecol_ref
  3.4 169.9 %shard_map.103 = (bf16[128,2048]{1,0:T(8,128)(2,1)}, bf16[2,2048,640]{2,1,0:T(8,128)(2,1)}, bf16[2,640,2048]{2,1,0:T(8,128)(2,1)}) custom-call(bf16[128,2048]{1,0:T(8,128)(2,1)} %tok_ref.1, bf16[128,2048]{1,0:T(8,128)(2,1)} %cot_ref.1, f32[128,1]{1,0:T(8,128)} %copy.11.gate_ref, s32[128,1]{1,0:T(8,128)} %copy.12.ecol_ref, s32[1,128]{1,0:T(1,128)} %bitcast.5, ...), custom_call_target="tpu_custom_call" | custom-call | flops 20132659200 | bytes 20971520 | tf_op jit(solution)/shard_map/pallas_call | solution.py:444
  173.3 0.0 slice-start
  173.3 2.0 %copy.16 = bf16[128,2048]{1,0:T(8,128)(2,1)} copy(bf16[128,2048]{1,0:T(8,128)(2,1)} %get-tuple-element.6) | data formatting | bytes 1048576
  175.4 0.0 slice-start.1
  175.4 5.4 %copy.17 = bf16[2,2048,640]{2,1,0:T(8,128)(2,1)} copy(bf16[2,2048,640]{2,1,0:T(8,128)(2,1)} %get-tuple-element.7) | data formatting | bytes 10485760
  180.8 0.0 slice-done
  180.8 0.0 slice-done.1
  180.8 2.4 %copy.18 = bf16[2,640,2048]{2,1,0:T(8,128)(2,1)} copy(bf16[2,640,2048]{2,1,0:T(8,128)(2,1)S(1)} %bitcast.3) | data formatting | bytes 10485760
  (1 shorter events, 0.0 us)
Async XLA Ops:
  173.3 7.4 %slice-start = ((s8[5242880]{0:T(1024)(128)(4,1)}), s8[4194304]{0:T(1024)(128)(4,1)S(1)}, s32[]{:S(2)}) async-start(s8[5242880]{0:T(1024)(128)(4,1)} %bitcast.2), calls=%async_computation | async-start | bytes 8388608
  175.4 5.4 %slice-start.1 = ((s8[5242880]{0:T(1024)(128)(4,1)}), s8[1048576]{0:T(1024)(128)(4,1)S(1)}, s32[]{:S(2)}) async-start(s8[5242880]{0:T(1024)(128)(4,1)} %bitcast.2), calls=%async_computation.1 | async-start | bytes 2097152

commit v2 on v0

v2 whole, which is shorter than its diff:
```python
import functools

import jax
import jax.numpy as jnp
import numpy as np
from jax import lax
from jax.experimental import pallas as pl
from jax.experimental.pallas import tpu as pltpu
from jax.sharding import PartitionSpec as P

ROOT = 0.7978845608028654
CUBIC = 0.044715
BF = jnp.bfloat16
F32 = jnp.float32
MESH = pl.DeviceIdType.MESH
CAP = 6
LOCAL = 2
SLOT = 16
NG = 16
NX = 4
ND = 8
HALF = NG * CAP
ROWS = LOCAL * HALF

ARRAY = ("rz", "rr", "rl", "hr", "hl", "xp1", "xm1", "xp1z", "xm1z", "fp1", "fm1", "fp1z", "fm1z", "z20", "z2m", "z2p", "z22")
BACK = ("a0", "a1", "b0", "b1", "c0", "c1", "d0", "d1", "q0", "q1", "q2", "q3", "s0", "s1", "t0", "t1", "z")
NAMES = (
    *("x" + n for n in ARRAY), *("c" + n for n in ARRAY), *("b" + n for n in BACK), "iz", "ir", "il", "if"
)


def gelu_pair(p):
    s = jnp.tanh(ROOT * (p + CUBIC * p * p * p))
    value = 0.5 * p * (1.0 + s)
    slope = 0.5 * (1.0 + s) + 0.5 * p * (1.0 - s * s) * ROOT * (1.0 + 3.0 * CUBIC * p * p)
    return value, slope


def dot(a, b):
    return jnp.dot(a, b, preferred_element_type=F32)


def dot_nt(a, b):
    return lax.dot_general(a, b, (((1,), (1,)), ((), ())), preferred_element_type=F32)


def dot_tn(a, b):
    return lax.dot_general(a, b, (((0,), (0,)), ((), ())), preferred_element_type=F32)


def kernel(
    c1, c2,
    tok_ref, cot_ref, gate_ref, erow_ref, pack_ref, spread_ref, win_hbm, wout_hbm,
    out_ref, win, wout,
    slots, u1, u2, v1, v2, s7, s6, x7, x6, y7, y6, b7, b6,
    gx1, gx2, gc1, gc2, hid, bh, p1, p2,
    ra, rb, rc, rd, rz, q1, qs0, qs1, qt0, qt1, w1, w2,
    wsem, a_send, a_recv, n_send, n_recv,
):
    e = lax.axis_index("expert")
    d = lax.axis_index("dp")
    zhi = e // 8
    x = d // 2
    zlo = d % 2
    zot = 1 - zlo
    xr = (x + 1) % NX
    xl = (x + 3) % NX
    xf = (x + 2) % NX
    zp = x * 2 + zot
    dxr = xr * 2 + zlo
    dxl = xl * 2 + zlo
    dxf = xf * 2 + zlo
    right, left, pair, far = (e, dxr), (e, dxl), (e, zp), (e, dxf)
    n_tok, width = tok_ref.shape
    n_exp = NG * LOCAL
    n_slot = NG * SLOT

    def group_dev(g):
        cross = (zhi + g // 8) % 2
        return (g, x * 2 + (zlo + cross) % 2)

    bar = pltpu.get_barrier_semaphore()

    def greet(k, carry):
        pl.semaphore_signal(bar, inc=1, device_id=group_dev((e + k) % NG), device_id_type=MESH)
        return carry

    for dev in (right, left, pair, far):
        pl.semaphore_signal(bar, inc=1, device_id=dev, device_id_type=MESH)
    lax.fori_loop(1, NG, greet, 0)

    load_in = pltpu.make_async_copy(win_hbm, win, wsem.at[0])
    load_out = pltpu.make_async_copy(wout_hbm, wout, wsem.at[1])
    load_in.start()
    load_out.start()

    erow = erow_ref[...]
    one_row = (lax.broadcasted_iota(jnp.int32, (n_exp, n_tok), 0) == erow).astype(F32)
    before = (
        lax.broadcasted_iota(jnp.int32, (n_tok, n_tok), 0)
        < lax.broadcasted_iota(jnp.int32, (n_tok, n_tok), 1)
    ).astype(F32)
    rank = jnp.sum(dot(one_row.astype(BF), before.astype(BF)) * one_row, axis=0, keepdims=True)
    slot_row = (erow >> 1) * SLOT + (erow & 1) * CAP + rank.astype(jnp.int32)
    slots[pl.ds(d, 1)] = jnp.broadcast_to(slot_row, (8, n_tok)).reshape(1, 8, n_tok)
    eye = lax.broadcasted_iota(jnp.int32, (n_tok, n_tok), 0) == lax.broadcasted_iota(jnp.int32, (n_tok, n_tok), 1)

    def column(row):
        return jnp.sum(jnp.where(eye, row, jnp.zeros_like(row)), axis=1, keepdims=True)

    def put(b):
        row = slots[b][:1]
        return (lax.broadcasted_iota(jnp.int32, (n_slot, n_tok), 0) == row).astype(F32).astype(BF)

    def take(b):
        col = column(slots[b][:1])
        return (lax.broadcasted_iota(jnp.int32, (n_tok, n_slot), 1) == col).astype(F32).astype(BF)

    gate = column(gate_ref[...])
    u1[pl.ds(zlo, 1)] = tok_ref[:, :c1].reshape(1, n_tok, c1)
    u2[pl.ds(x, 1)] = tok_ref[:, c1:].reshape(1, n_tok, c2)
    v1[pl.ds(zlo, 1)] = (gate * cot_ref[:, :c1].astype(F32)).astype(BF).reshape(1, n_tok, c1)
    v2[pl.ds(x, 1)] = (gate * cot_ref[:, c1:].astype(F32)).astype(BF).reshape(1, n_tok, c2)

    sent = []

    def go(name, src, dst, dev):
        i = NAMES.index(name)
        cp = pltpu.make_async_remote_copy(
            src_ref=src, dst_ref=dst, send_sem=n_send.at[i], recv_sem=n_recv.at[i], device_id=dev, device_id_type=MESH
        )
        cp.start()
        sent.append(cp)

    def got(name, dst):
        i = NAMES.index(name)
        pltpu.make_async_remote_copy(
            src_ref=dst, dst_ref=dst, send_sem=n_send.at[i], recv_sem=n_recv.at[i], device_id=pair, device_id_type=MESH
        ).wait_recv()

    def across(j, src, dst):
        return pltpu.make_async_remote_copy(
            src_ref=src, dst_ref=dst, send_sem=a_send.at[j], recv_sem=a_recv.at[j], device_id=pair, device_id_type=MESH
        )

    def scatter_out(j, src, dst, value):
        src[...] = value.astype(BF).reshape(src.shape)
        dst[pl.ds(e, 1)] = src[pl.ds(e, 1)]

        def one(k, carry):
            g = (e + k) % NG
            pltpu.make_async_remote_copy(
                src_ref=src.at[g], dst_ref=dst.at[e], send_sem=a_send.at[j], recv_sem=a_recv.at[j],
                device_id=group_dev(g), device_id_type=MESH,
            ).start()
            return carry

        lax.fori_loop(1, NG, one, 0)

    others = pl.ds(0, NG - 1)

    def scatter_in(j, src, dst):
        across(j, src.at[others], dst.at[others]).wait_recv()
        return dst[...].reshape(n_slot, dst.shape[-1])

    def scatter_sent(j, src, dst):
        across(j, src.at[others], dst.at[others]).wait_send()

    lo, hi = pl.ds(0, HALF), pl.ds(HALF, HALF)
    tlo, thi = pl.ds(0, n_tok // 2), pl.ds(n_tok // 2, n_tok // 2)
    row_x = (x, xl, xr, xf)

    class Array:
        def __init__(self, i, tag, raw1, raw2, a7, a6, g1, g2):
            self.i, self.tag = i, tag
            self.raw1, self.raw2, self.a7, self.a6, self.g1, self.g2 = raw1, raw2, a7, a6, g1, g2

        def go(self, name, ref, dev):
            go(self.tag + name, ref, ref, dev)

        def got(self, name, ref):
            got(self.tag + name, ref)

        def raw(self):
            self.go("rr", self.raw2.at[x], right)
            self.go("rl", self.raw2.at[x], left)
            self.go("rz", self.raw1.at[zlo], pair)

        def free(self, b):
            if self.i > 0:
                scatter_sent(6 * self.i - 6 + b, s7.at[b] if b < 2 else s6.at[b - 2], b7.at[b] if b < 2 else b6.at[b - 2])

        def own1(self):
            self.free(0)
            scatter_out(6 * self.i, s7.at[0], self.a7.at[0], dot(put(d), self.raw1[zlo]))

        def own2(self):
            self.free(2)
            scatter_out(6 * self.i + 2, s6.at[0], self.a6.at[0], dot(put(d), self.raw2[x]))

        def pair1(self):
            self.got("rz", self.raw1.at[zot])
            self.free(1)
            scatter_out(6 * self.i + 1, s7.at[1], self.a7.at[1], dot(put(zp), self.raw1[zot]))

        def pass_on(self):
            self.got("rr", self.raw2.at[xl])
            self.go("hr", self.raw2.at[xl, tlo], right)
            self.got("rl", self.raw2.at[xr])
            self.go("hl", self.raw2.at[xr, thi], left)

        def near2(self):
            for b, xi in ((1, xl), (2, xr)):
                self.free(2 + b)
                scatter_out(6 * self.i + 2 + b, s6.at[b], self.a6.at[b], dot(put(xi * 2 + zlo), self.raw2[xi]))

        def far2(self):
            self.got("hr", self.raw2.at[xf, tlo])
            self.got("hl", self.raw2.at[xf, thi])
            self.free(5)
            scatter_out(6 * self.i + 5, s6.at[3], self.a6.at[3], dot(put(dxf), self.raw2[xf]))

        def land1(self, b):
            rows = scatter_in(6 * self.i + b, s7.at[b], self.a7.at[b])
            at = (d, zp)[b]
            self.g1[pl.ds(at, 1)] = dot(pack_ref[...], rows).astype(BF).reshape(1, ROWS, c1)
            self.go(("xp1", "xp1z")[b], self.g1.at[at], right)
            self.go(("xm1", "xm1z")[b], self.g1.at[at], left)

        def land2(self, b):
            rows = scatter_in(6 * self.i + 2 + b, s6.at[b], self.a6.at[b])
            at = row_x[b] * 2 + zlo
            self.g2[pl.ds(at, 1)] = dot(pack_ref[...], rows).astype(BF).reshape(1, ROWS, c2)
            self.go(("z20", "z2m", "z2p", "z22")[b], self.g2.at[at], pair)

        def ring(self, b):
            g1, z, t = self.g1, (zlo, zot)[b], ("", "z")[b]
            self.got("xp1" + t, g1.at[xl * 2 + z])
            self.go("fp1" + t, g1.at[xl * 2 + z, lo], right)
            self.got("xm1" + t, g1.at[xr * 2 + z])
            self.go("fm1" + t, g1.at[xr * 2 + z, hi], left)

        def whole(self, b):
            if b == 3:
                for z, t in ((zlo, ""), (zot, "z")):
                    self.got("fp1" + t, self.g1.at[xf * 2 + z, lo])
                    self.got("fm1" + t, self.g1.at[xf * 2 + z, hi])
            self.got(("z20", "z2m", "z2p", "z22")[b], self.g2.at[row_x[b] * 2 + zot])

    def block(ref, xi, le):
        return ref[pl.ds(2 * xi, 2), pl.ds(pl.multiple_of(le * HALF, 32), HALF), :].reshape(2 * HALF, ref.shape[-1])

    def keep(ref, xi, le, value):
        ref[pl.ds(2 * xi, 2), pl.ds(pl.multiple_of(le * HALF, 32), HALF), :] = value.reshape(2, HALF, ref.shape[-1])

    def forward(xi):
        def one(le, carry):
            pre = dot(block(gx1, xi, le), win[le, :c1, :]) + dot(block(gx2, xi, le), win[le, c1:, :])
            value, slope = gelu_pair(pre)
            h = value.astype(BF)
            keep(hid, xi, le, h)
            keep(bh, xi, le, slope.astype(BF))
            keep(p1, xi, le, dot(h, wout[le, :, :c1]).astype(BF))
            keep(p2, xi, le, dot(h, wout[le, :, c1:]).astype(BF))
            return carry

        lax.fori_loop(0, LOCAL, one, 0)

    def backward(xi):
        def one(le, carry):
            b = dot_nt(block(gc1, xi, le), wout[le, :, :c1]) + dot_nt(block(gc2, xi, le), wout[le, :, c1:])
            keep(bh, xi, le, (b * block(bh, xi, le).astype(F32)).astype(BF))
            return carry

        lax.fori_loop(0, LOCAL, one, 0)

    def rows_of(ref, le, start, size):
        return ref[:, pl.ds(pl.multiple_of(le * HALF, 32), HALF), pl.ds(start, size)].reshape(ND * HALF, size)

    TILE = 128

    def grads_in(le):
        bhe = rows_of(bh, le, 0, bh.shape[-1])

        def first(i, carry):
            s = pl.multiple_of(i * (c1 // 3), TILE)
            win[le, pl.ds(s, c1 // 3), :] = dot_tn(rows_of(gx1, le, s, c1 // 3), bhe).astype(BF)
            return carry

        lax.fori_loop(0, 3, first, 0)
        win[le, c1:, :] = dot_tn(rows_of(gx2, le, 0, c2), bhe).astype(BF)

    def grads_out(le):
        def one(i, carry):
            s = pl.multiple_of(i * TILE, TILE)
            h = rows_of(hid, le, s, TILE)
            wout[le, pl.ds(s, TILE), :c1] = dot_tn(h, rows_of(gc1, le, 0, c1)).astype(BF)
            wout[le, pl.ds(s, TILE), c1:] = dot_tn(h, rows_of(gc2, le, 0, c2)).astype(BF)
            return carry

        lax.fori_loop(0, hid.shape[-1] // TILE, one, 0)

    def add(dst, src):
        dst[...] = (dst[...].astype(F32) + src[...].astype(F32)).astype(BF)

    zs = ((0, zlo), (1, zot))
    order = ((3, xf), (1, xl), (2, xr), (0, x))

    def back_first():
        for j, z in zs[::-1]:
            go(f"ba{j}", p1.at[xf * 2 + z, lo], ra.at[j], right)
            go(f"bb{j}", p1.at[xf * 2 + z, hi], rb.at[j], left)

    def back_pair(b, xi):
        go(f"bq{b}", p2.at[xi * 2 + zot], q1.at[b], pair)

    def back_second(j):
        z = (zlo, zot)[j]
        got(f"ba{j}", ra.at[j])
        add(p1.at[xr * 2 + z, lo], ra.at[j])
        go(f"bc{j}", p1.at[xr * 2 + z], rc.at[j], right)
        got(f"bb{j}", rb.at[j])
        add(p1.at[xl * 2 + z, hi], rb.at[j])
        go(f"bd{j}", p1.at[xl * 2 + z], rd.at[j], left)

    def back_third(j):
        got(f"bc{j}", rc.at[j])
        got(f"bd{j}", rd.at[j])
        total = p1[(d, zp)[j]].astype(F32) + rc[j].astype(F32) + rd[j].astype(F32)
        scatter_sent(6 + j, s7.at[j], y7.at[j])
        scatter_out(12 + j, s7.at[j], b7.at[j], dot(spread_ref[...], total.astype(BF)))

    def back_across(b, xi):
        got(f"bq{b}", q1.at[b])
        total = p2[xi * 2 + zlo].astype(F32) + q1[b].astype(F32)
        scatter_sent(8 + b, s6.at[b], y6.at[b])
        scatter_out(14 + b, s6.at[b], b6.at[b], dot(spread_ref[...], total.astype(BF)))

    def rows_back(b, at):
        if b < 2:
            return dot(take(at), scatter_in(12 + b, s7.at[b], b7.at[b]))
        return dot(take(at), scatter_in(12 + b, s6.at[b - 2], b6.at[b - 2]))

    def back_far():
        w2[0] = rows_back(5, dxf).astype(BF)
        go("bs0", w2.at[0, tlo], qs0, right)
        go("bs1", w2.at[0, thi], qs1, left)

    def back_near():
        w2[1] = rows_back(4, dxr).astype(BF)
        w2[2] = rows_back(3, dxl).astype(BF)
        got("bs0", qs0)
        add(w2.at[1, tlo], qs0)
        go("bt0", w2.at[1], qt0, right)
        got("bs1", qs1)
        add(w2.at[2, thi], qs1)
        go("bt1", w2.at[2], qt1, left)

    def back_own():
        mine = rows_back(2, d)
        got("bt0", qt0)
        got("bt1", qt1)
        out_ref[:, c1:] = (gate * (mine + qt0[...].astype(F32) + qt1[...].astype(F32))).astype(BF)

    def back_z():
        w1[...] = rows_back(1, zp).astype(BF)
        go("bz", w1, rz, pair)

    def back_z_own():
        mine = rows_back(0, d)
        got("bz", rz)
        out_ref[:, :c1] = (gate * (mine + rz[...].astype(F32))).astype(BF)

    X = Array(0, "x", u1, u2, x7, x6, gx1, gx2)
    C = Array(1, "c", v1, v2, y7, y6, gc1, gc2)

    pl.semaphore_wait(bar, NG - 1 + 4)
    go("iz", slots.at[d], slots.at[d], pair)
    go("ir", slots.at[d], slots.at[d], right)
    go("il", slots.at[d], slots.at[d], left)
    go("if", slots.at[d], slots.at[d], far)
    X.raw()
    X.own1()
    X.own2()
    C.raw()
    got("iz", slots.at[zp])
    X.pair1()
    got("ir", slots.at[dxl])
    got("il", slots.at[dxr])
    X.pass_on()
    X.near2()
    X.land1(0)
    X.land2(0)
    got("if", slots.at[dxf])
    X.far2()
    C.own1()
    X.land1(1)
    C.pair1()
    C.own2()
    C.pass_on()
    C.near2()
    X.ring(0)
    X.land2(1)
    X.land2(2)
    load_in.wait()
    load_out.wait()
    X.whole(0)
    forward(x)
    X.land2(3)
    C.far2()
    X.ring(1)
    C.land1(0)
    C.land1(1)
    C.land2(0)
    X.whole(1)
    forward(xl)
    X.whole(2)
    forward(xr)
    C.ring(0)
    C.land2(1)
    C.land2(2)
    X.whole(3)
    forward(xf)
    back_first()
    back_pair(*order[0])
    C.land2(3)
    C.ring(1)
    back_pair(*order[1])
    back_pair(*order[2])
    back_pair(*order[3])
    C.whole(0)
    backward(x)
    C.whole(1)
    backward(xl)
    C.whole(2)
    backward(xr)
    back_across(*order[0])
    back_second(1)
    back_second(0)
    C.whole(3)
    backward(xf)
    back_far()
    grads_in(0)
    back_across(*order[1])
    back_third(1)
    back_across(*order[2])
    back_third(0)
    grads_in(1)
    back_near()
    back_across(*order[3])
    back_z()
    grads_out(0)
    grads_out(1)
    back_own()
    back_z_own()

    for b in range(6):
        scatter_sent(12 + b, s7.at[b] if b < 2 else s6.at[b - 2], b7.at[b] if b < 2 else b6.at[b - 2])
    for cp in sent:
        cp.wait_send()


def shards(tokens, cotangent, gate_prob, expert_of, w_in, w_out):
    n_tok, width = tokens.shape
    ff = w_in.shape[-1]
    c1 = width * 9 // 16
    c2 = width - c1
    o = np.arange(ROWS)
    source = (o % HALF) // CAP * SLOT + o // HALF * CAP + o % CAP
    pack = (np.arange(NG * SLOT)[None, :] == source[:, None]).astype(np.float32)
    vm = pl.BlockSpec(memory_space=pltpu.VMEM)
    hbm = pl.BlockSpec(memory_space=pl.ANY)

    def buf(*shape):
        return pltpu.VMEM(shape, BF)

    sevens = [buf(2, NG, SLOT, c1), buf(NX, NG, SLOT, c2)]
    raws = [buf(2, n_tok, c1), buf(NX, n_tok, c2)]
    gathered = [buf(ND, ROWS, c1), buf(ND, ROWS, c2)]
    return pl.pallas_call(
        functools.partial(kernel, c1, c2),
        out_shape=(
            pltpu.VMEM(tokens.shape, BF),
            pltpu.VMEM(w_in.shape, BF),
            pltpu.VMEM(w_out.shape, BF),
        ),
        in_specs=[vm] * 6 + [hbm] * 2,
        out_specs=(vm, vm, vm),
        scratch_shapes=[
            pltpu.VMEM((ND, 8, n_tok), jnp.int32),
            *raws, *raws,
            *sevens, *sevens, *sevens, *sevens,
            *gathered, *gathered,
            buf(ND, ROWS, ff), buf(ND, ROWS, ff),
            *gathered,
            buf(2, HALF, c1), buf(2, HALF, c1), buf(2, ROWS, c1), buf(2, ROWS, c1), buf(n_tok, c1),
            buf(NX, ROWS, c2), buf(n_tok // 2, c2), buf(n_tok // 2, c2), buf(n_tok, c2), buf(n_tok, c2),
            buf(n_tok, c1), buf(3, n_tok, c2),
            pltpu.SemaphoreType.DMA((2,)),
            pltpu.SemaphoreType.DMA((18,)), pltpu.SemaphoreType.DMA((18,)),
            pltpu.SemaphoreType.DMA((len(NAMES),)), pltpu.SemaphoreType.DMA((len(NAMES),)),
        ],
        compiler_params=pltpu.CompilerParams(collective_id=0, has_side_effects=True, vmem_limit_bytes=50 << 20),
        cost_estimate=pl.CostEstimate(
            flops=10 * ND * ROWS * width * ff, bytes_accessed=8 * w_in.size, transcendentals=ND * ROWS * ff
        ),
    )(
        tokens, cotangent, gate_prob.reshape(1, n_tok), expert_of.reshape(1, n_tok),
        jnp.asarray(pack, BF), jnp.asarray(pack.T, BF), w_in, w_out,
    )


def solution(mesh):
    return jax.shard_map(
        shards,
        mesh=mesh,
        in_specs=(
            P(("expert", "dp"), None),
            P(("expert", "dp"), None),
            P(("expert", "dp")),
            P(("expert", "dp"), None),
            P("expert", None, "dp"),
            P("expert", "dp", None),
        ),
        out_specs=(P(("expert", "dp"), None), P("expert", None, "dp"), P("expert", "dp", None)),
        check_vma=False,
    )
```

time: 370 us -> 149 us (0.40); the launches traced: 363 us -> 149 us
  waiting for transfers between devices: 179 us -> 0 us
  Pallas kernels: 0 us -> 143 us
  local copies, waits for them, and re-layouts: 81.5 us -> 5.51 us
  matrix products: 49.9 us -> 0 us
  starting transfers between devices: 31.8 us -> 0 us
  other arithmetic: 20.2 us -> 0 us
    all_to_all x3 -> x0, waiting for transfers between devices: 179 us -> none  [the longest x1 100 us: shards(): lax.all_to_all(wide_x, ('expert', 'dp'), split_axis=0, concat_axis=0, til...]
    pallas_call x0 -> x1, Pallas kernels: none -> 143 us  [shards(): pl.pallas_call(functools.partial(kernel, c1, c2), out_shape=(pltpu.VMEM(t...]
    dot_general x8 -> x0, matrix products: 49.9 us -> none  [the longest x2 23 us: run_expert(): lax.dot_general(rows_x, back_hidden, (((0,), (0,)), ((), ())), preferred_...]
    all_to_all x3 -> x0, starting transfers between devices: 31.8 us -> none  [the longest x1 12 us: shards(): lax.all_to_all(wide_x, ('expert', 'dp'), split_axis=0, concat_axis=0, til...]
    another operation x6 -> x0, local copies, waits for them, and re-layouts: 30.1 us -> none  [the longest x2 12.9 us: shards(): rows_z = slots_z[:, slot_index].reshape(senders * capacity, model_width)]
    slice x6 -> x0, local copies, waits for them, and re-layouts: 17.3 us -> none  [the longest x3 8.66 us: shards(): rows_x = slots_x[:, slot_index].reshape(senders * capacity, model_width)]
    all_to_all x2 -> x0, local copies, waits for them, and re-layouts: 13.7 us -> none  [the longest x1 6.83 us: shards(): lax.all_to_all(wide_x, ('expert', 'dp'), split_axis=0, concat_axis=0, til...]
    broadcast_in_dim x4 -> x0, local copies, waits for them, and re-layouts: 8.92 us -> none  [the longest x2 4.46 us: shards(): jnp.broadcast_to(send_x.reshape(groups, 1, slot_count, model_width), (gro...]
  transfers between devices with their start and end apart: 3 -> 0, of which waited for: 3 -> 0; matrix products, arithmetic and copies ran while one was open for 35% -> 0% of each run, Pallas kernels for 0% -> 0%
where the time goes in v2:
time: 149 us
  Pallas kernels  143 us (96%)
  local copies, waits for them, and re-layouts  5.51 us (4%)
    pallas_call x1, Pallas kernels, shards(): pl.pallas_call(functools.partial(kernel, c1, c2), out_shape=(pltpu.VMEM(t...  143 us
    unnamed x3, local copies, waits for them, and re-layouts  5.51 us

profile of v2, /device:TPU:1, one launch (start us, length us, event | category | flops | bytes accessed | tf_op | source)
XLA Modules:
  0.0 149.1 jit_solution(6386331677429463538)
XLA Ops:
  0.6 142.9 %shard_map.103 = (bf16[128,2048]{1,0:T(8,128)(2,1)S(1)}, bf16[2,2048,640]{2,1,0:T(8,128)(2,1)S(1)}, bf16[2,640,2048]{2,1,0:T(8,128)(2,1)S(1)}) custom-call(bf16[128,2048]{1,0:T(8,128)(2,1)} %tok_ref.1, bf16[128,2048]{1,0:T(8,128)(2,1)} %cot_ref.1, f32[1,128]{1,0:T(1,128)} %bitcast.2, s32[1,128]{1,0:T(1,128)} %bitcast.3, ...), custom_call_target="tpu_custom_call" | custom-call | flops 20132659200 | bytes 20971520 | tf_op jit(solution)/shard_map/pallas_call | solution.py:480
  143.6 0.8 copy.14
  144.4 2.4 %copy.15 = bf16[2,2048,640]{2,1,0:T(8,128)(2,1)} copy(bf16[2,2048,640]{2,1,0:T(8,128)(2,1)S(1)} %get-tuple-element.4) | data formatting | bytes 10485760
  146.7 2.4 %copy.16 = bf16[2,640,2048]{2,1,0:T(8,128)(2,1)} copy(bf16[2,640,2048]{2,1,0:T(8,128)(2,1)S(1)} %get-tuple-element.5) | data formatting | bytes 10485760

commit v3 on v2

--- a/solution.py
+++ b/solution.py
@@ -181,9 +181,11 @@
         def got(self, name, ref):
             got(self.tag + name, ref)
 
-        def raw(self):
+        def raw_x(self):
             self.go("rr", self.raw2.at[x], right)
             self.go("rl", self.raw2.at[x], left)
+
+        def raw_z(self):
             self.go("rz", self.raw1.at[zlo], pair)
 
         def free(self, b):
@@ -203,16 +205,18 @@
             self.free(1)
             scatter_out(6 * self.i + 1, s7.at[1], self.a7.at[1], dot(put(zp), self.raw1[zot]))
 
-        def pass_on(self):
+        def pass_right(self):
             self.got("rr", self.raw2.at[xl])
             self.go("hr", self.raw2.at[xl, tlo], right)
+
+        def pass_left(self):
             self.got("rl", self.raw2.at[xr])
             self.go("hl", self.raw2.at[xr, thi], left)
 
-        def near2(self):
-            for b, xi in ((1, xl), (2, xr)):
-                self.free(2 + b)
-                scatter_out(6 * self.i + 2 + b, s6.at[b], self.a6.at[b], dot(put(xi * 2 + zlo), self.raw2[xi]))
+        def near2(self, b):
+            xi = row_x[b]
+            self.free(2 + b)
+            scatter_out(6 * self.i + 2 + b, s6.at[b], self.a6.at[b], dot(put(xi * 2 + zlo), self.raw2[xi]))
 
         def far2(self):
             self.got("hr", self.raw2.at[xf, tlo])
@@ -233,10 +237,13 @@
             self.g2[pl.ds(at, 1)] = dot(pack_ref[...], rows).astype(BF).reshape(1, ROWS, c2)
             self.go(("z20", "z2m", "z2p", "z22")[b], self.g2.at[at], pair)
 
-        def ring(self, b):
+        def ring_right(self, b):
             g1, z, t = self.g1, (zlo, zot)[b], ("", "z")[b]
             self.got("xp1" + t, g1.at[xl * 2 + z])
             self.go("fp1" + t, g1.at[xl * 2 + z, lo], right)
+
+        def ring_left(self, b):
+            g1, z, t = self.g1, (zlo, zot)[b], ("", "z")[b]
             self.got("xm1" + t, g1.at[xr * 2 + z])
             self.go("fm1" + t, g1.at[xr * 2 + z, hi], left)
 
@@ -275,43 +282,33 @@
         lax.fori_loop(0, LOCAL, one, 0)
 
     def rows_of(ref, le, start, size):
-        return ref[:, pl.ds(pl.multiple_of(le * HALF, 32), HALF), pl.ds(start, size)].reshape(ND * HALF, size)
-
-    TILE = 128
-
-    def grads_in(le):
+        return ref[:, pl.ds(le * HALF, HALF), pl.ds(start, size)].reshape(ND * HALF, size)
+
+    def grads_in(le, part):
         bhe = rows_of(bh, le, 0, bh.shape[-1])
-
-        def first(i, carry):
-            s = pl.multiple_of(i * (c1 // 3), TILE)
-            win[le, pl.ds(s, c1 // 3), :] = dot_tn(rows_of(gx1, le, s, c1 // 3), bhe).astype(BF)
-            return carry
-
-        lax.fori_loop(0, 3, first, 0)
-        win[le, c1:, :] = dot_tn(rows_of(gx2, le, 0, c2), bhe).astype(BF)
-
-    def grads_out(le):
-        def one(i, carry):
-            s = pl.multiple_of(i * TILE, TILE)
-            h = rows_of(hid, le, s, TILE)
-            wout[le, pl.ds(s, TILE), :c1] = dot_tn(h, rows_of(gc1, le, 0, c1)).astype(BF)
-            wout[le, pl.ds(s, TILE), c1:] = dot_tn(h, rows_of(gc2, le, 0, c2)).astype(BF)
-            return carry
-
-        lax.fori_loop(0, hid.shape[-1] // TILE, one, 0)
+        if part == 0:
+            win[le, :c1, :] = dot_tn(rows_of(gx1, le, 0, c1), bhe).astype(BF)
+        else:
+            win[le, c1:, :] = dot_tn(rows_of(gx2, le, 0, c2), bhe).astype(BF)
+
+    def grads_out(le, part):
+        h = rows_of(hid, le, 0, hid.shape[-1])
+        if part == 0:
+            wout[le, :, :c1] = dot_tn(h, rows_of(gc1, le, 0, c1)).astype(BF)
+        else:
+            wout[le, :, c1:] = dot_tn(h, rows_of(gc2, le, 0, c2)).astype(BF)
 
     def add(dst, src):
         dst[...] = (dst[...].astype(F32) + src[...].astype(F32)).astype(BF)
 
     zs = ((0, zlo), (1, zot))
-    order = ((3, xf), (1, xl), (2, xr), (0, x))
-
     def back_first():
         for j, z in zs[::-1]:
             go(f"ba{j}", p1.at[xf * 2 + z, lo], ra.at[j], right)
             go(f"bb{j}", p1.at[xf * 2 + z, hi], rb.at[j], left)
 
-    def back_pair(b, xi):
+    def back_pair(b):
+        xi = row_x[b]
         go(f"bq{b}", p2.at[xi * 2 + zot], q1.at[b], pair)
 
     def back_second(j):
@@ -330,7 +327,8 @@
         scatter_sent(6 + j, s7.at[j], y7.at[j])
         scatter_out(12 + j, s7.at[j], b7.at[j], dot(spread_ref[...], total.astype(BF)))
 
-    def back_across(b, xi):
+    def back_across(b):
+        xi = row_x[b]
         got(f"bq{b}", q1.at[b])
         total = p2[xi * 2 + zlo].astype(F32) + q1[b].astype(F32)
         scatter_sent(8 + b, s6.at[b], y6.at[b])
@@ -346,12 +344,14 @@
         go("bs0", w2.at[0, tlo], qs0, right)
         go("bs1", w2.at[0, thi], qs1, left)
 
-    def back_near():
+    def back_right():
         w2[1] = rows_back(4, dxr).astype(BF)
-        w2[2] = rows_back(3, dxl).astype(BF)
         got("bs0", qs0)
         add(w2.at[1, tlo], qs0)
         go("bt0", w2.at[1], qt0, right)
+
+    def back_left():
+        w2[2] = rows_back(3, dxl).astype(BF)
         got("bs1", qs1)
         add(w2.at[2, thi], qs1)
         go("bt1", w2.at[2], qt1, left)
@@ -379,80 +379,95 @@
     go("ir", slots.at[d], slots.at[d], right)
     go("il", slots.at[d], slots.at[d], left)
     go("if", slots.at[d], slots.at[d], far)
-    X.raw()
+    X.raw_x()
     X.own1()
+    X.raw_z()
     X.own2()
-    C.raw()
+    C.raw_x()
+    X.pass_right()
     got("iz", slots.at[zp])
     X.pair1()
+    C.raw_z()
+    X.pass_left()
+    X.land1(0)
     got("ir", slots.at[dxl])
+    X.near2(1)
+    C.pass_right()
     got("il", slots.at[dxr])
-    X.pass_on()
-    X.near2()
-    X.land1(0)
+    X.near2(2)
+    C.pass_left()
     X.land2(0)
     got("if", slots.at[dxf])
     X.far2()
-    C.own1()
     X.land1(1)
     C.pair1()
-    C.own2()
-    C.pass_on()
-    C.near2()
-    X.ring(0)
+    X.ring_left(0)
     X.land2(1)
-    X.land2(2)
+    X.ring_right(0)
     load_in.wait()
     load_out.wait()
     X.whole(0)
     forward(x)
+    X.land2(2)
+    X.ring_left(1)
     X.land2(3)
-    C.far2()
-    X.ring(1)
-    C.land1(0)
+    C.own1()
+    X.ring_right(1)
     C.land1(1)
-    C.land2(0)
+    C.near2(2)
     X.whole(1)
     forward(xl)
+    back_pair(1)
+    C.own2()
     X.whole(2)
     forward(xr)
-    C.ring(0)
-    C.land2(1)
+    C.land1(0)
+    C.near2(1)
     C.land2(2)
     X.whole(3)
     forward(xf)
     back_first()
-    back_pair(*order[0])
-    C.land2(3)
-    C.ring(1)
-    back_pair(*order[1])
-    back_pair(*order[2])
-    back_pair(*order[3])
+    C.far2()
+    C.land2(0)
+    back_pair(2)
+    back_across(1)
+    back_pair(3)
+    back_second(1)
+    C.ring_left(0)
+    back_second(0)
+    C.land2(1)
     C.whole(0)
     backward(x)
+    C.ring_left(1)
+    C.ring_right(1)
+    back_across(2)
+    C.land2(3)
+    C.whole(2)
+    backward(xr)
+    back_third(1)
+    back_pair(0)
+    back_across(3)
+    C.ring_right(0)
     C.whole(1)
     backward(xl)
-    C.whole(2)
-    backward(xr)
-    back_across(*order[0])
-    back_second(1)
-    back_second(0)
+    back_far()
+    back_z()
+    back_third(0)
     C.whole(3)
     backward(xf)
-    back_far()
-    grads_in(0)
-    back_across(*order[1])
-    back_third(1)
-    back_across(*order[2])
-    back_third(0)
-    grads_in(1)
-    back_near()
-    back_across(*order[3])
-    back_z()
-    grads_out(0)
-    grads_out(1)
+    grads_out(0, 0)
+    grads_out(1, 0)
+    back_left()
+    back_right()
+    grads_in(0, 0)
+    back_across(0)
+    grads_out(0, 1)
+    grads_in(1, 1)
+    grads_in(0, 1)
+    grads_in(1, 0)
+    grads_out(1, 1)
+    back_z_own()
     back_own()
-    back_z_own()
 
     for b in range(6):
         scatter_sent(12 + b, s7.at[b] if b < 2 else s6.at[b - 2], b7.at[b] if b < 2 else b6.at[b - 2])

time: 149 us -> 138 us (0.926)
  Pallas kernels: 143 us -> 132 us
    pallas_call x1, Pallas kernels: 143 us -> 132 us  [shards(): pl.pallas_call(functools.partial(kernel, c1, c2), out_shape=(pltpu.VMEM(t...]
where the time goes in v3:
time: 138 us
  Pallas kernels  132 us (96%)
  local copies, waits for them, and re-layouts  5.51 us (4%)
    pallas_call x1, Pallas kernels, shards(): pl.pallas_call(functools.partial(kernel, c1, c2), out_shape=(pltpu.VMEM(t...  132 us
    unnamed x3, local copies, waits for them, and re-layouts  5.51 us

profile of v3, /device:TPU:1, one launch (start us, length us, event | category | flops | bytes accessed | tf_op | source)
XLA Modules:
  0.0 137.8 jit_solution(15917159576176218642)
XLA Ops:
  0.6 131.7 %shard_map.103 = (bf16[128,2048]{1,0:T(8,128)(2,1)S(1)}, bf16[2,2048,640]{2,1,0:T(8,128)(2,1)S(1)}, bf16[2,640,2048]{2,1,0:T(8,128)(2,1)S(1)}) custom-call(bf16[128,2048]{1,0:T(8,128)(2,1)} %tok_ref.1, bf16[128,2048]{1,0:T(8,128)(2,1)} %cot_ref.1, f32[1,128]{1,0:T(1,128)} %bitcast.2, s32[1,128]{1,0:T(1,128)} %bitcast.3, ...), custom_call_target="tpu_custom_call" | custom-call | flops 20132659200 | bytes 20971520 | tf_op jit(solution)/shard_map/pallas_call | solution.py:495
  132.3 0.8 copy.14
  133.1 2.4 %copy.15 = bf16[2,2048,640]{2,1,0:T(8,128)(2,1)} copy(bf16[2,2048,640]{2,1,0:T(8,128)(2,1)S(1)} %get-tuple-element.4) | data formatting | bytes 10485760
  135.5 2.4 %copy.16 = bf16[2,640,2048]{2,1,0:T(8,128)(2,1)} copy(bf16[2,640,2048]{2,1,0:T(8,128)(2,1)S(1)} %get-tuple-element.5) | data formatting | bytes 10485760

commit v4 on v3

--- a/solution.py
+++ b/solution.py
@@ -51,8 +51,8 @@
 def kernel(
     c1, c2,
     tok_ref, cot_ref, gate_ref, erow_ref, pack_ref, spread_ref, win_hbm, wout_hbm,
-    out_ref, win, wout,
-    slots, u1, u2, v1, v2, s7, s6, x7, x6, y7, y6, b7, b6,
+    out_ref, win, gout,
+    wout, slots, u1, u2, v1, v2, s7, s6, x7, x6, y7, y6, b7, b6,
     gx1, gx2, gc1, gc2, hid, bh, p1, p2,
     ra, rb, rc, rd, rz, q1, qs0, qs1, qt0, qt1, w1, w2,
     wsem, a_send, a_recv, n_send, n_recv,
@@ -281,22 +281,26 @@
 
         lax.fori_loop(0, LOCAL, one, 0)
 
-    def rows_of(ref, le, start, size):
-        return ref[:, pl.ds(le * HALF, HALF), pl.ds(start, size)].reshape(ND * HALF, size)
+    def early(ref, le):
+        return jnp.concatenate([block(ref, xi, le) for xi in (x, xl, xr)], axis=0)
+
+    parts = ((pl.ds(0, c1), gx1, gc1), (pl.ds(c1, c2), gx2, gc2))
 
     def grads_in(le, part):
-        bhe = rows_of(bh, le, 0, bh.shape[-1])
-        if part == 0:
-            win[le, :c1, :] = dot_tn(rows_of(gx1, le, 0, c1), bhe).astype(BF)
-        else:
-            win[le, c1:, :] = dot_tn(rows_of(gx2, le, 0, c2), bhe).astype(BF)
+        at, gx, _ = parts[part]
+        win[le, at, :] = dot_tn(early(gx, le), early(bh, le)).astype(BF)
 
     def grads_out(le, part):
-        h = rows_of(hid, le, 0, hid.shape[-1])
-        if part == 0:
-            wout[le, :, :c1] = dot_tn(h, rows_of(gc1, le, 0, c1)).astype(BF)
-        else:
-            wout[le, :, c1:] = dot_tn(h, rows_of(gc2, le, 0, c2)).astype(BF)
+        at, _, gc = parts[part]
+        gout[le, :, at] = dot_tn(early(hid, le), early(gc, le)).astype(BF)
+
+    def last_in(le, part):
+        at, gx, _ = parts[part]
+        win[le, at, :] = (win[le, at, :].astype(F32) + dot_tn(block(gx, xf, le), block(bh, xf, le))).astype(BF)
+
+    def last_out(le, part):
+        at, _, gc = parts[part]
+        gout[le, :, at] = (gout[le, :, at].astype(F32) + dot_tn(block(hid, xf, le), block(gc, xf, le))).astype(BF)
 
     def add(dst, src):
         dst[...] = (dst[...].astype(F32) + src[...].astype(F32)).astype(BF)
@@ -381,91 +385,99 @@
     go("if", slots.at[d], slots.at[d], far)
     X.raw_x()
     X.own1()
+    C.raw_x()
     X.raw_z()
     X.own2()
-    C.raw_x()
     X.pass_right()
+    C.raw_z()
+    X.land1(0)
+    X.pass_left()
+    got("il", slots.at[dxr])
+    X.near2(2)
     got("iz", slots.at[zp])
     X.pair1()
-    C.raw_z()
-    X.pass_left()
-    X.land1(0)
+    X.land2(0)
     got("ir", slots.at[dxl])
     X.near2(1)
+    X.land2(2)
+    X.ring_left(0)
     C.pass_right()
-    got("il", slots.at[dxr])
-    X.near2(2)
-    C.pass_left()
-    X.land2(0)
+    X.land1(1)
     got("if", slots.at[dxf])
     X.far2()
-    X.land1(1)
-    C.pair1()
-    X.ring_left(0)
+    X.ring_right(0)
     X.land2(1)
-    X.ring_right(0)
+    C.own1()
+    C.near2(1)
+    C.pass_left()
+    C.own2()
+    X.land2(3)
+    C.near2(2)
+    X.ring_left(1)
+    X.ring_right(1)
     load_in.wait()
     load_out.wait()
-    X.whole(0)
-    forward(x)
-    X.land2(2)
-    X.ring_left(1)
-    X.land2(3)
-    C.own1()
-    X.ring_right(1)
-    C.land1(1)
-    C.near2(2)
     X.whole(1)
     forward(xl)
     back_pair(1)
-    C.own2()
+    C.land1(0)
+    X.whole(3)
+    forward(xf)
+    back_pair(3)
+    back_first()
+    C.pair1()
+    C.land2(0)
     X.whole(2)
     forward(xr)
-    C.land1(0)
-    C.near2(1)
+    C.land1(1)
+    back_second(1)
+    C.far2()
     C.land2(2)
-    X.whole(3)
-    forward(xf)
-    back_first()
-    C.far2()
-    C.land2(0)
+    X.whole(0)
+    forward(x)
+    C.land2(1)
     back_pair(2)
+    back_second(0)
+    C.ring_right(0)
+    back_across(3)
     back_across(1)
-    back_pair(3)
-    back_second(1)
     C.ring_left(0)
-    back_second(0)
-    C.land2(1)
     C.whole(0)
     backward(x)
+    back_far()
     C.ring_left(1)
-    C.ring_right(1)
-    back_across(2)
-    C.land2(3)
+    back_pair(0)
     C.whole(2)
     backward(xr)
-    back_third(1)
-    back_pair(0)
-    back_across(3)
-    C.ring_right(0)
+    C.ring_right(1)
     C.whole(1)
     backward(xl)
-    back_far()
+    back_third(1)
+    grads_in(1, 1)
+    C.land2(3)
+    grads_in(0, 1)
+    grads_out(1, 1)
+    back_across(2)
+    grads_out(1, 0)
+    grads_in(0, 0)
+    back_third(0)
+    grads_out(0, 1)
+    grads_out(0, 0)
     back_z()
-    back_third(0)
+    back_right()
+    back_across(0)
+    grads_in(1, 0)
+    back_left()
     C.whole(3)
     backward(xf)
-    grads_out(0, 0)
-    grads_out(1, 0)
-    back_left()
-    back_right()
-    grads_in(0, 0)
-    back_across(0)
-    grads_out(0, 1)
-    grads_in(1, 1)
-    grads_in(0, 1)
-    grads_in(1, 0)
-    grads_out(1, 1)
+    last_in(0, 1)
+    last_in(1, 1)
+    last_out(1, 0)
+    last_out(0, 1)
+    last_in(0, 0)
+    last_out(0, 0)
+    last_in(1, 0)
+    last_out(1, 1)
     back_z_own()
     back_own()
 
@@ -502,6 +514,7 @@
         in_specs=[vm] * 6 + [hbm] * 2,
         out_specs=(vm, vm, vm),
         scratch_shapes=[
+            buf(*w_out.shape),
             pltpu.VMEM((ND, 8, n_tok), jnp.int32),
             *raws, *raws,
             *sevens, *sevens, *sevens, *sevens,
@@ -515,7 +528,7 @@
             pltpu.SemaphoreType.DMA((18,)), pltpu.SemaphoreType.DMA((18,)),
             pltpu.SemaphoreType.DMA((len(NAMES),)), pltpu.SemaphoreType.DMA((len(NAMES),)),
         ],
-        compiler_params=pltpu.CompilerParams(collective_id=0, has_side_effects=True, vmem_limit_bytes=50 << 20),
+        compiler_params=pltpu.CompilerParams(collective_id=0, has_side_effects=True, vmem_limit_bytes=53 << 20),
         cost_estimate=pl.CostEstimate(
             flops=10 * ND * ROWS * width * ff, bytes_accessed=8 * w_in.size, transcendentals=ND * ROWS * ff
         ),

time: 138 us -> 133 us (0.964)
  Pallas kernels: 132 us -> 127 us
    pallas_call x1, Pallas kernels: 132 us -> 127 us  [shards(): pl.pallas_call(functools.partial(kernel, c1, c2), out_shape=(pltpu.VMEM(t...]
where the time goes in v4:
time: 133 us
  Pallas kernels  127 us (95%)
  local copies, waits for them, and re-layouts  5.51 us (4%)
    pallas_call x1, Pallas kernels, shards(): pl.pallas_call(functools.partial(kernel, c1, c2), out_shape=(pltpu.VMEM(t...  127 us
    unnamed x3, local copies, waits for them, and re-layouts  5.51 us

profile of v4, /device:TPU:1, one launch (start us, length us, event | category | flops | bytes accessed | tf_op | source)
XLA Modules:
  0.0 132.7 jit_solution(13862573241160397737)
XLA Ops:
  0.6 126.5 %shard_map.103 = (bf16[128,2048]{1,0:T(8,128)(2,1)S(1)}, bf16[2,2048,640]{2,1,0:T(8,128)(2,1)S(1)}, bf16[2,640,2048]{2,1,0:T(8,128)(2,1)S(1)}) custom-call(bf16[128,2048]{1,0:T(8,128)(2,1)} %tok_ref.1, bf16[128,2048]{1,0:T(8,128)(2,1)} %cot_ref.1, f32[1,128]{1,0:T(1,128)} %bitcast.2, s32[1,128]{1,0:T(1,128)} %bitcast.3, ...), custom_call_target="tpu_custom_call" | custom-call | flops 20132659200 | bytes 20971520 | tf_op jit(solution)/shard_map/pallas_call | solution.py:507
  127.2 0.8 copy.14
  128.0 2.4 %copy.15 = bf16[2,2048,640]{2,1,0:T(8,128)(2,1)} copy(bf16[2,2048,640]{2,1,0:T(8,128)(2,1)S(1)} %get-tuple-element.4) | data formatting | bytes 10485760
  130.3 2.4 %copy.16 = bf16[2,640,2048]{2,1,0:T(8,128)(2,1)} copy(bf16[2,640,2048]{2,1,0:T(8,128)(2,1)S(1)} %get-tuple-element.5) | data formatting | bytes 10485760

commit v5 on v4

--- a/solution.py
+++ b/solution.py
@@ -383,101 +383,101 @@
     go("ir", slots.at[d], slots.at[d], right)
     go("il", slots.at[d], slots.at[d], left)
     go("if", slots.at[d], slots.at[d], far)
+    C.raw_z()
     X.raw_x()
     X.own1()
+    X.own2()
     C.raw_x()
     X.raw_z()
-    X.own2()
+    X.land1(0)
     X.pass_right()
-    C.raw_z()
-    X.land1(0)
-    X.pass_left()
-    got("il", slots.at[dxr])
-    X.near2(2)
+    got("ir", slots.at[dxl])
+    X.near2(1)
     got("iz", slots.at[zp])
     X.pair1()
     X.land2(0)
-    got("ir", slots.at[dxl])
-    X.near2(1)
-    X.land2(2)
+    X.pass_left()
+    C.pass_left()
+    X.ring_right(0)
+    got("il", slots.at[dxr])
+    X.near2(2)
+    X.land2(1)
+    X.land1(1)
     X.ring_left(0)
-    C.pass_right()
-    X.land1(1)
     got("if", slots.at[dxf])
     X.far2()
-    X.ring_right(0)
-    X.land2(1)
+    X.land2(2)
     C.own1()
-    C.near2(1)
-    C.pass_left()
     C.own2()
+    C.pass_right()
+    C.pair1()
     X.land2(3)
-    C.near2(2)
+    X.ring_right(1)
     X.ring_left(1)
-    X.ring_right(1)
     load_in.wait()
     load_out.wait()
     X.whole(1)
     forward(xl)
     back_pair(1)
     C.land1(0)
+    X.whole(2)
+    forward(xr)
+    C.near2(2)
+    C.near2(1)
+    back_pair(2)
     X.whole(3)
     forward(xf)
-    back_pair(3)
     back_first()
-    C.pair1()
-    C.land2(0)
-    X.whole(2)
-    forward(xr)
-    C.land1(1)
-    back_second(1)
-    C.far2()
-    C.land2(2)
     X.whole(0)
     forward(x)
+    C.land2(2)
+    C.land2(0)
+    C.land1(1)
+    C.far2()
+    back_across(2)
+    back_second(1)
     C.land2(1)
-    back_pair(2)
+    C.whole(0)
+    backward(x)
+    back_pair(3)
     back_second(0)
-    C.ring_right(0)
-    back_across(3)
+    C.land2(3)
     back_across(1)
     C.ring_left(0)
-    C.whole(0)
-    backward(x)
-    back_far()
+    C.ring_right(0)
+    C.ring_right(1)
     C.ring_left(1)
-    back_pair(0)
     C.whole(2)
     backward(xr)
-    C.ring_right(1)
     C.whole(1)
     backward(xl)
+    back_pair(0)
     back_third(1)
+    grads_out(1, 0)
+    grads_out(1, 1)
+    grads_in(0, 1)
+    back_across(3)
+    grads_out(0, 1)
     grads_in(1, 1)
-    C.land2(3)
-    grads_in(0, 1)
-    grads_out(1, 1)
-    back_across(2)
-    grads_out(1, 0)
     grads_in(0, 0)
     back_third(0)
-    grads_out(0, 1)
     grads_out(0, 0)
+    back_far()
     back_z()
+    grads_in(1, 0)
+    C.whole(3)
+    backward(xf)
     back_right()
     back_across(0)
-    grads_in(1, 0)
     back_left()
-    C.whole(3)
-    backward(xf)
+    last_out(1, 0)
+    last_in(1, 1)
+    last_in(0, 0)
+    last_out(1, 1)
     last_in(0, 1)
-    last_in(1, 1)
-    last_out(1, 0)
+    last_in(1, 0)
+    last_out(0, 0)
     last_out(0, 1)
-    last_in(0, 0)
-    last_out(0, 0)
-    last_in(1, 0)
-    last_out(1, 1)
     back_z_own()
     back_own()
 

time: 133 us -> 136 us (1.023)
  Pallas kernels: 127 us -> 129 us
    pallas_call x1, Pallas kernels: 127 us -> 129 us  [shards(): pl.pallas_call(functools.partial(kernel, c1, c2), out_shape=(pltpu.VMEM(t...]
where the time goes in v5:
time: 136 us
  Pallas kernels  129 us (95%)
  local copies, waits for them, and re-layouts  5.51 us (4%)
    pallas_call x1, Pallas kernels, shards(): pl.pallas_call(functools.partial(kernel, c1, c2), out_shape=(pltpu.VMEM(t...  129 us
    unnamed x3, local copies, waits for them, and re-layouts  5.51 us

profile of v5, /device:TPU:1, one launch (start us, length us, event | category | flops | bytes accessed | tf_op | source)
XLA Modules:
  0.0 135.6 jit_solution(8028776778407852536)
XLA Ops:
  0.6 129.4 %shard_map.103 = (bf16[128,2048]{1,0:T(8,128)(2,1)S(1)}, bf16[2,2048,640]{2,1,0:T(8,128)(2,1)S(1)}, bf16[2,640,2048]{2,1,0:T(8,128)(2,1)S(1)}) custom-call(bf16[128,2048]{1,0:T(8,128)(2,1)} %tok_ref.1, bf16[128,2048]{1,0:T(8,128)(2,1)} %cot_ref.1, f32[1,128]{1,0:T(1,128)} %bitcast.2, s32[1,128]{1,0:T(1,128)} %bitcast.3, ...), custom_call_target="tpu_custom_call" | custom-call | flops 20132659200 | bytes 20971520 | tf_op jit(solution)/shard_map/pallas_call | solution.py:507
  130.1 0.8 copy.14
  130.9 2.4 %copy.15 = bf16[2,2048,640]{2,1,0:T(8,128)(2,1)} copy(bf16[2,2048,640]{2,1,0:T(8,128)(2,1)S(1)} %get-tuple-element.4) | data formatting | bytes 10485760
  133.2 2.4 %copy.16 = bf16[2,640,2048]{2,1,0:T(8,128)(2,1)} copy(bf16[2,640,2048]{2,1,0:T(8,128)(2,1)S(1)} %get-tuple-element.5) | data formatting | bytes 10485760
